TPU v7x, 256 devices: a whole 4x4x8 slice. The times are simulated.
256 devices in a mesh: prefix: 32 (over z, y), sample: 8 (over x, core).
Axes of the slice: x: 4, y: 4, z: 8, core: 2. Of those that a mesh axis runs over, the one named last changes fastest.
Arguments:
- residual: bfloat16 [512, 5376], P(('prefix', 'sample')), may hold values from -6 to 6
- queries: bfloat16 [512, 4096], P(('prefix', 'sample')), may hold values from -133 to 133
- fresh_key_value: bfloat16 [512, 2, 2048], P(('prefix', 'sample')), may hold values from -5 to 5
- prompt_key_value: bfloat16 [16, 2, 4096, 2048], P('sample', None, 'prefix'), may hold values from -5 to 5
- suffix_key_value: bfloat16 [512, 2, 192, 2048], P(('prefix', 'sample')), may hold values from -5 to 5
- suffix_len: int32 [512], P(('prefix', 'sample')), may hold values from 1 to 192, 49152 in all
- sample_prompt: int32 [512], replicated, may hold values from 0 to 15, as said below
- out_weight: bfloat16 [4096, 5376], P('prefix'), may hold values from -0.09375 to 0.09375
- attn_gain: float32 [5376], replicated, may hold values from 0.5 to 1.5
- ffn_gain: float32 [5376], replicated, may hold values from 0.5 to 1.5
- gate_weight: bfloat16 [5376, 21504], P('sample', 'prefix'), may hold values from -0.15625 to 0.15625
- up_weight: bfloat16 [5376, 21504], P('sample', 'prefix'), may hold values from -0.15625 to 0.15625
- down_weight: bfloat16 [21504, 5376], P('prefix', 'sample'), may hold values from -0.078125 to 0.078125
Outputs:
- midway: bfloat16 [512, 5376], P(('prefix', 'sample'))
- ffn_out: bfloat16 [512, 5376], P('prefix', 'sample')
Inputs may be any that keep to these rules, and one draw needn't show every extreme that they name: `sample_prompt`: sample s belongs to prompt 2 j or 2 j + 1, with j = (s // 2) % 8; each prompt has exactly 32 samples.
All inputs are finite; a program needn't handle non-finite values. No bound on the sum of `suffix_len` on one device may be relied on, other than what follows from the above.
Results may differ from a plain program's by a relative error of at most 0.025.
Values may be sent and summed in bfloat16 or wider, within the bound.
A program may use at most 64 MiB of HBM per device.

v0:
```python
import jax
import jax.numpy as jnp
from jax import lax
from jax.sharding import PartitionSpec as P

QUERY_HEADS = 32
KEY_VALUE_HEADS = 16
HEAD_WIDTH = 128


SCALE = 168.0 ** (-0.5)
NEGATIVE = -1e30
EPSILON = 1e-06


def soft_pieces(logit_scores, values, pattern):
    row_max = jnp.max(logit_scores, axis=-1)
    expo = jnp.exp(logit_scores - row_max[..., None])
    totals = jnp.sum(expo, axis=-1)
    weights = expo.astype(jnp.bfloat16)
    blended = jnp.einsum(pattern, weights, values, preferred_element_type=jnp.float32)
    return (blended, row_max, totals)


def rms_scale(values, gain_vec):
    mean_square = jnp.mean(values * values, axis=-1, keepdims=True)
    return values * lax.rsqrt(mean_square + EPSILON) * gain_vec


def local(
    residual,
    queries,
    fresh_key_value,
    prompt_key_value,
    suffix_key_value,
    suffix_len,
    sample_prompt,
    out_weight,
    attn_gain,
    ffn_gain,
    gate_weight,
    up_weight,
    down_weight,
):
    n_prefix = lax.axis_size("prefix")
    n_sample = lax.axis_size("sample")
    prefix_pos = lax.axis_index("prefix")
    sample_pos = lax.axis_index("sample")
    owned_count = queries.shape[0]
    group_list = QUERY_HEADS // KEY_VALUE_HEADS
    paired_count = prompt_key_value.shape[0]
    stretch_factor = prompt_key_value.shape[2]
    queries_by_row = lax.all_gather(queries, "prefix", axis=0, tiled=True)
    count_of_rows = queries_by_row.shape[0]
    lookup = sample_prompt.reshape(n_prefix, n_sample, owned_count)
    row_prompt = (
        lax.dynamic_index_in_dim(lookup, sample_pos, 1, keepdims=False).reshape(count_of_rows)
        - paired_count * sample_pos
    )
    grouped_query = queries_by_row.reshape(count_of_rows, KEY_VALUE_HEADS, group_list, HEAD_WIDTH)
    key_tile = prompt_key_value[:, 0].reshape(
        paired_count, stretch_factor, KEY_VALUE_HEADS, HEAD_WIDTH
    )
    value_tile = prompt_key_value[:, 1].reshape(
        paired_count, stretch_factor, KEY_VALUE_HEADS, HEAD_WIDTH
    )
    logit_scores = (
        jnp.einsum("rkgd,pnkd->rkgpn", grouped_query, key_tile, preferred_element_type=jnp.float32)
        * SCALE
    )
    chosen = row_prompt[:, None] == jnp.arange(paired_count, dtype=jnp.int32)[None, :]
    logit_scores = jnp.where(chosen[:, None, None, :, None], logit_scores, NEGATIVE).reshape(
        count_of_rows, KEY_VALUE_HEADS, group_list, paired_count * stretch_factor
    )
    blended, row_max, totals = soft_pieces(
        logit_scores,
        value_tile.reshape(paired_count * stretch_factor, KEY_VALUE_HEADS, HEAD_WIDTH),
        "awul,lwc->awuc",
    )
    blended = blended.reshape(count_of_rows, QUERY_HEADS, HEAD_WIDTH)
    row_max = row_max.reshape(count_of_rows, QUERY_HEADS)
    totals = totals.reshape(count_of_rows, QUERY_HEADS)
    owned_query = queries.reshape(owned_count, KEY_VALUE_HEADS, group_list, HEAD_WIDTH)
    suffix_extent = suffix_key_value.shape[2]
    tail_keys = jnp.concatenate(
        [suffix_key_value[:, 0], fresh_key_value[:, 0][:, None]], axis=1
    ).reshape(owned_count, suffix_extent + 1, KEY_VALUE_HEADS, HEAD_WIDTH)
    tail_values = jnp.concatenate(
        [suffix_key_value[:, 1], fresh_key_value[:, 1][:, None]], axis=1
    ).reshape(owned_count, suffix_extent + 1, KEY_VALUE_HEADS, HEAD_WIDTH)
    tail_scores = (
        jnp.einsum("skgd,snkd->skgn", owned_query, tail_keys, preferred_element_type=jnp.float32)
        * SCALE
    )
    slot_index = jnp.arange(suffix_extent + 1, dtype=jnp.int32)
    usable = (slot_index[None, :] < suffix_len[:, None]) | (slot_index[None, :] == suffix_extent)
    tail_scores = jnp.where(usable[:, None, None, :], tail_scores, NEGATIVE)
    tail_blend, tail_max, tail_totals = soft_pieces(tail_scores, tail_values, "skgn,snkd->skgd")
    offset = prefix_pos * owned_count
    head_blend = lax.dynamic_slice_in_dim(blended, offset, owned_count, 0)
    head_max = lax.dynamic_slice_in_dim(row_max, offset, owned_count, 0)
    head_totals = lax.dynamic_slice_in_dim(totals, offset, owned_count, 0)
    tail_max = tail_max.reshape(owned_count, QUERY_HEADS)
    joint_max = jnp.maximum(head_max, tail_max)
    prior_scale = jnp.exp(head_max - joint_max)
    tail_scale = jnp.exp(tail_max - joint_max)
    joined = (
        head_blend * prior_scale[..., None]
        + tail_blend.reshape(owned_count, QUERY_HEADS, HEAD_WIDTH) * tail_scale[..., None]
    )
    joined_totals = (
        head_totals * prior_scale + tail_totals.reshape(owned_count, QUERY_HEADS) * tail_scale
    )
    blended = lax.dynamic_update_slice_in_dim(blended, joined, offset, 0)
    row_max = lax.dynamic_update_slice_in_dim(row_max, joint_max, offset, 0)
    totals = lax.dynamic_update_slice_in_dim(totals, joined_totals, offset, 0)
    pieces, maxima, sum_parts = (
        lax.all_to_all(blended[None], "prefix", split_axis=2, concat_axis=0, tiled=True),
        lax.all_to_all(row_max[None], "prefix", split_axis=2, concat_axis=0, tiled=True),
        lax.all_to_all(totals[None], "prefix", split_axis=2, concat_axis=0, tiled=True),
    )
    global_max = jnp.max(maxima, axis=0)
    factor = jnp.exp(maxima - global_max[None])
    numerator = jnp.sum(pieces * factor[..., None], axis=0)
    denominator = jnp.sum(sum_parts * factor, axis=0)
    attended = (numerator / denominator[..., None]).astype(jnp.bfloat16).reshape(count_of_rows, -1)
    projected = lax.psum_scatter(
        jnp.dot(attended, out_weight, preferred_element_type=jnp.float32),
        "prefix",
        scatter_dimension=0,
        tiled=True,
    )
    midway = (residual.astype(jnp.float32) + rms_scale(projected, attn_gain)).astype(jnp.bfloat16)
    settled = lax.optimization_barrier(midway).astype(jnp.float32)
    ffn_in = rms_scale(settled, ffn_gain).astype(jnp.bfloat16)
    slice_width = ffn_in.shape[1] // n_sample
    everything = lax.all_gather(ffn_in, ("prefix", "sample"), axis=0, tiled=True)
    columns = lax.dynamic_slice_in_dim(everything, sample_pos * slice_width, slice_width, 1)
    gate_part = jnp.dot(columns, gate_weight, preferred_element_type=jnp.float32)
    up_part = jnp.dot(columns, up_weight, preferred_element_type=jnp.float32)
    gate_sum, up_sum = lax.psum((gate_part, up_part), "sample")
    hidden = (jax.nn.gelu(gate_sum, approximate=True) * up_sum).astype(jnp.bfloat16)
    ffn_out = lax.psum_scatter(
        jnp.dot(hidden, down_weight, preferred_element_type=jnp.float32),
        "prefix",
        scatter_dimension=0,
        tiled=True,
    ).astype(jnp.bfloat16)
    return (midway, ffn_out)


def solution(mesh):
    return jax.shard_map(
        local,
        mesh=mesh,
        in_specs=(
            P(("prefix", "sample"), None),
            P(("prefix", "sample"), None),
            P(("prefix", "sample"), None, None),
            P("sample", None, "prefix", None),
            P(("prefix", "sample"), None, None, None),
            P(("prefix", "sample")),
            P(),
            P("prefix", None),
            P(),
            P(),
            P("sample", "prefix"),
            P("sample", "prefix"),
            P("prefix", "sample"),
        ),
        out_specs=(P(("prefix", "sample"), None), P("prefix", "sample")),
        check_vma=False,
    )
```

profile of v0, /device:TPU:1, one launch (start us, length us, event | category | flops | bytes accessed | tf_op | source)
XLA Modules:
  0.0 737.2 jit_solution(9845411049398798678)
XLA Ops:
  11.1 42.3 %all-gather = bf16[32,2,4096]{2,1,0:T(2,128)(2,1)S(1)} all-gather(bf16[1,2,4096]{2,1,0:T(2,128)(2,1)} %bitcast.100), channel_id=1, replica_groups=mesh['prefix'=32,'sample'=8] {'prefix'}, dimensions={0}, use_global_device_ids=true | all-gather | bytes 540672 | tf_op jit(solution)/shard_map/all_gather | solution.py:53
  54.6 2.7 fusion.65
  58.6 2.6 fusion.66
  61.2 2.0 exponential_reduce_fusion
  65.3 3.4 fusion.64
  77.1 5.1 all-to-all-start.2
  82.2 3.0 copy.59
  86.0 2.5 copy.86
  88.5 2.9 reshape.237
  91.4 1.8 copy.88
  97.6 1.5 dynamic_update_slice.13
  99.1 13.2 %all-to-all-start.1 = ((f32[1,64,32]{1,0,2:T(1,128)}), f32[1,64,32]{1,0,2:T(1,128)S(1)}, u32[]{:S(2)}, u32[]{:S(2)}) async-start(f32[1,64,32]{1,0,2:T(1,128)} %dynamic_update_slice.13), calls=%async_computation.1 | async-start | bytes 32768 | tf_op jit(solution)/shard_map/all_to_all | solution.py:119
  113.1 7.8 %all-to-all-done.1 = f32[1,64,32]{1,0,2:T(1,128)S(1)} async-done(((f32[1,64,32]{1,0,2:T(1,128)}), f32[1,64,32]{1,0,2:T(1,128)S(1)}, u32[]{:S(2)}, u32[]{:S(2)}) %all-to-all-start.1) | async-done | bytes 8224 | tf_op jit(solution)/shard_map/all_to_all | solution.py:119
  120.8 4.1 all-to-all-start
  125.1 17.4 %all-to-all-done = f32[1,64,32,128]{3,1,0,2:T(8,128)S(1)} async-done(((f32[1,64,32,128]{3,1,0,2:T(8,128)}), f32[1,64,32,128]{3,1,0,2:T(8,128)S(1)}, u32[]{:S(2)}, u32[]{:S(2)}) %all-to-all-start) | async-done | bytes 1048608 | tf_op jit(solution)/shard_map/all_to_all | solution.py:118
  142.9 1.5 fusion.51
  145.7 157.0 %all-reduce.5.cloned.1.call-done = f32[64,5376]{1,0:T(8,128)} async-done(((f32[64,5376]{1,0:T(8,128)}), f32[64,5376]{1,0:T(8,128)}) %all-reduce.5.cloned.1.call-update) | async-done | bytes 1376272
  305.9 119.9 %all-gather.4.cloned.1.call-done = bf16[256,2,5376]{2,1,0:T(2,128)(2,1)} async-done(((bf16[1,2,5376]{2,1,0:T(2,128)(2,1)}), bf16[256,2,5376]{2,1,0:T(2,128)(2,1)}) %all-gather.4.cloned.1.call-update) | async-done | bytes 5505040 | tf_op jit(solution)/shard_map/all_gather | solution.py:137
  425.8 11.7 %reshape.248 = bf16[512,5376]{1,0:T(8,128)(2,1)} reshape(bf16[256,2,5376]{2,1,0:T(2,128)(2,1)} %all-gather.4.cloned.1.call-done) | data formatting | bytes 11010048
  437.5 3.4 fusion.31
  440.9 3.2 fusion.33
  444.2 68.1 %all-reduce.7.cloned.1.call-done = (f32[512,672]{0,1:T(8,128)}, f32[512,672]{0,1:T(8,128)}) async-done(((f32[512,672]{0,1:T(8,128)}, f32[512,672]{0,1:T(8,128)}), (f32[512,672]{0,1:T(8,128)}, f32[512,672]{0,1:T(8,128)})) %all-reduce.7.cloned.1.call-update) | async-done | bytes 2752528 | tf_op jit(solution)/shard_map/psum | solution.py:141
  512.3 3.9 fusion.35
  516.2 213.0 %reduce-scatter.2.cloned.1.call-done = f32[16,672]{1,0:T(8,128)} async-done(((f32[512,672]{1,0:T(8,128)}), f32[16,672]{1,0:T(8,128)}) %reduce-scatter.2.cloned.1.call-update) | async-done | bytes 43024 | tf_op jit(solution)/shard_map/reduce_scatter | solution.py:143
  (95 shorter events, 28.4 us)
Async XLA Ops:
  7.2 135.7 %copy-start = (bf16[128,5376]{1,0:T(8,128)(2,1)S(1)}, bf16[128,5376]{1,0:T(8,128)(2,1)}, u32[]{:S(2)}) copy-start(bf16[128,5376]{1,0:T(8,128)(2,1)} %param.20) | copy-start | bytes 4128772
  70.9 4.2 copy-start.5
  70.9 11.3 %copy-start.3 = (f32[2,16,2,193]{3,2,1,0:T(2,128)}, f32[2,16,2,193]{3,2,1,0:T(2,128)S(1)}, u32[]{:S(2)}) copy-start(f32[2,16,2,193]{3,2,1,0:T(2,128)S(1)} %get-tuple-element.17) | copy-start | bytes 148228
  77.1 22.0 %all-to-all-start.2 = ((f32[1,64,32]{1,0,2:T(1,128)}), f32[1,64,32]{1,0,2:T(1,128)S(1)}, u32[]{:S(2)}, u32[]{:S(2)}) async-start(f32[1,64,32]{1,0,2:T(1,128)} %bitcast.27), calls=%async_computation.2 | async-start | bytes 32768 | tf_op jit(solution)/shard_map/all_to_all | solution.py:120
  93.7 1.2 copy-start.1
  94.9 0.9 copy-start.6
  94.9 0.9 copy-start.11
  96.4 1.0 copy-start.15
  96.4 1.1 copy-start.14
  96.4 1.2 copy-start.13
  99.1 21.7 %all-to-all-start.1 = ((f32[1,64,32]{1,0,2:T(1,128)}), f32[1,64,32]{1,0,2:T(1,128)S(1)}, u32[]{:S(2)}, u32[]{:S(2)}) async-start(f32[1,64,32]{1,0,2:T(1,128)} %dynamic_update_slice.13), calls=%async_computation.1 | async-start | bytes 32768 | tf_op jit(solution)/shard_map/all_to_all | solution.py:119
  120.8 21.7 %all-to-all-start = ((f32[1,64,32,128]{3,1,0,2:T(8,128)}), f32[1,64,32,128]{3,1,0,2:T(8,128)S(1)}, u32[]{:S(2)}, u32[]{:S(2)}) async-start(f32[1,64,32,128]{3,1,0,2:T(8,128)} %bitcast_dynamic-update-slice_fusion), calls=%async_computation | async-start | bytes 2097152 | tf_op jit(solution)/shard_map/all_to_all | solution.py:118
  124.9 177.8 %all-reduce.5.cloned.1.call-start = ((), (), s32[]{:S(2)}) async-start(), calls=%async_computation.6 | async-start | bytes 2752512
  142.9 1.6 copy-start.20
  142.9 161.0 %copy-start.7 = (f32[5376]{0:T(1024)S(1)}, f32[5376]{0:T(1024)}, u32[]{:S(2)}) copy-start(f32[5376]{0:T(1024)} %param.21) | copy-start | bytes 64516
  142.9 161.0 %copy-start.9 = (bf16[2,5376]{1,0:T(2,128)(2,1)S(1)}, bf16[2,5376]{1,0:T(2,128)(2,1)}, u32[]{:S(2)}) copy-start(bf16[2,5376]{1,0:T(2,128)(2,1)} %param.13) | copy-start | bytes 64516
  142.9 162.2 %copy-start.8 = (f32[5376]{0:T(1024)S(1)}, f32[5376]{0:T(1024)}, u32[]{:S(2)}) copy-start(f32[5376]{0:T(1024)} %param.22) | copy-start | bytes 64516
  144.4 281.3 %all-gather.4.cloned.1.call-start = ((), (), s32[]{:S(2)}) async-start(), calls=%async_computation.5 | async-start | bytes 5526528 | tf_op jit(solution)/shard_map/all_gather | solution.py:137
  304.9 132.6 %copy-start.2 = (bf16[2,5376]{1,0:T(2,128)(2,1)}, bf16[2,5376]{1,0:T(2,128)(2,1)S(1)}, u32[]{:S(2)}) copy-start(bf16[2,5376]{1,0:T(2,128)(2,1)S(1)} %add_convert_fusion) | copy-start | bytes 64516
  305.8 206.5 %all-reduce.7.cloned.1.call-start = ((), (), s32[]{:S(2)}) async-start(), calls=%async_computation.7 | async-start | bytes 5505024 | tf_op jit(solution)/shard_map/psum | solution.py:141
  305.9 131.6 %copy-start.17 = (bf16[672,672]{1,0:T(8,128)(2,1)S(1)}, bf16[672,672]{1,0:T(8,128)(2,1)}, u32[]{:S(2)}) copy-start(bf16[672,672]{1,0:T(8,128)(2,1)} %param.24) | copy-start | bytes 2709508
  437.5 3.4 copy-start.18
  444.1 68.2 %copy-start.19 = (bf16[672,672]{1,0:T(8,128)(2,1)S(1)}, bf16[672,672]{1,0:T(8,128)(2,1)}, u32[]{:S(2)}) copy-start(bf16[672,672]{1,0:T(8,128)(2,1)} %param.25) | copy-start | bytes 2709508
  444.1 285.1 %reduce-scatter.2.cloned.1.call-start = ((), (), s32[]{:S(2)}) async-start(), calls=%async_computation.4 | async-start | bytes 1622016 | tf_op jit(solution)/shard_map/reduce_scatter | solution.py:143
  (4 other events, 3.0 us)
Sparse Core Ops, SparseCore 0:
  144.6 158.1 all-reduce.4
  307.8 117.9 all-gather.3
  444.2 68.0 all-reduce.6
  516.3 212.8 reduce-scatter.1
where the time goes:
time: 743 us; the launch traced here: 737 us
  waiting for transfers between devices  583 us (78%)
  local copies, waits for them, and re-layouts  47.1 us (6%)
  blocking collectives  42.3 us (6%)
  starting transfers between devices  22.6 us (3%)
  matrix products  17.1 us (2%)
  between operations  14.7 us (2%)
  other arithmetic  10.1 us (1%)
    reduce_scatter x1, waiting for transfers between devices, local(): lax.psum_scatter(jnp.dot(hidden, down_weight, preferred_element_type=jnp....  213 us
    unnamed x5, waiting for transfers between devices  157 us
    all_gather x1, waiting for transfers between devices, local(): lax.all_gather(ffn_in, ('prefix', 'sample'), axis=0, tiled=True)  120 us
    psum x1, waiting for transfers between devices, local(): gate_sum, up_sum = lax.psum((gate_part, up_part), 'sample')  68.1 us
    all_gather x1, blocking collectives, local(): queries_by_row = lax.all_gather(queries, 'prefix', axis=0, tiled=True)  42.3 us
    unnamed x51, local copies, waits for them, and re-layouts  21.7 us
    all_to_all x1, waiting for transfers between devices, local(): lax.all_to_all(blended[None], 'prefix', split_axis=2, concat_axis=0, tile...  17.4 us
  transfers between devices with their start and end apart: 7, of which 6 were waited for; matrix products, arithmetic and copies ran while one was open for 2% of the time, Pallas kernels for 0%

commit v1 on v0

v1 whole, which is shorter than its diff:
```python
import functools

import jax
import jax.numpy as jnp
from jax import lax
from jax.experimental import pallas as pl
from jax.experimental.pallas import tpu as pltpu
from jax.sharding import PartitionSpec as P

MESH = pl.DeviceIdType.MESH
SCALE = 168.0 ** (-0.5)
NEGATIVE = -1e30
EPSILON = 1e-06
BF = jnp.bfloat16
F32 = jnp.float32

NZ, NY, NX, NC = 8, 4, 4, 2
NP, NS = NZ * NY, NX * NC
HEADS, KV, WIDTH = 32, 16, 128
D = 5376
CHUNKS = D // 128
PROJ_ROWS = 88
BLOCK = 672
SUF = 192
SUFX = 208
Y_OFFSETS = (1, 3, 2)


def dot(a, b):
    return jnp.dot(a, b, preferred_element_type=F32)


def dot_t(a, b):
    return lax.dot_general(a, b, (((1,), (1,)), ((), ())), preferred_element_type=F32)


def remote(src, dst, send_sem, recv_sem, device):
    return pltpu.make_async_remote_copy(
        src_ref=src,
        dst_ref=dst,
        send_sem=send_sem,
        recv_sem=recv_sem,
        device_id=device,
        device_id_type=MESH,
    )


def body(
    q_ref,
    fresh_ref,
    resid_ref,
    again_ref,
    fgain_ref,
    slen_ref,
    sprompt_ref,
    pkv_hbm,
    skv_hbm,
    wout_hbm,
    wg_hbm,
    wu_hbm,
    wd_hbm,
    mid_ref,
    out_ref,
    pkv,
    skv,
    wout,
    wg,
    wu,
    wd,
    load_sem,
    q32,
    qall,
    qflat,
    sel,
    ssuf,
    msufx,
    lsufx,
    osufx,
    stat,
    osend,
    orecv,
    stsend,
    strecv,
    pf,
    psend,
    precv,
    gains,
    resid,
    e1send,
    e1recv,
    e1f,
    xf,
    xall,
    gu,
    gurecv,
    xs,
    xsrecv,
    hid,
    ysend,
    yrecv,
    zsend,
    zrecv,
    aq_z,
    aq_y,
    c_o,
    c_st,
    d_p,
    e_1,
    e_z,
    e_y,
    f_c,
    f_x,
    f_hx,
    f_hc,
    g_y,
    g_z,
):
    me = lax.axis_index("prefix")
    spos = lax.axis_index("sample")
    z, y = me // NY, me % NY
    x, c = spos // NC, spos % NC

    def at_prefix(p):
        return {"prefix": p, "sample": spos}

    def at_zy(zz, yy):
        return {"prefix": zz * NY + yy, "sample": spos}

    def at_sample(s):
        return {"prefix": me, "sample": s}

    def at_xc(xx, cc):
        return {"prefix": me, "sample": xx * NC + cc}

    loads = []

    def load(src, dst):
        cp = pltpu.make_async_copy(src, dst, load_sem.at[len(loads)])
        cp.start()
        loads.append(cp)

    for s in range(2):
        for t in range(2):
            load(skv_hbm.at[s, t], skv.at[s, t, pl.ds(0, SUF)])
    load(pkv_hbm, pkv)
    load(wout_hbm, wout)
    load(wg_hbm, wg)
    load(wu_hbm, wu)
    load(wd_hbm, wd)

    barrier = pltpu.get_barrier_semaphore()

    @pl.loop(1, NP)
    def _(i):
        pl.semaphore_signal(
            barrier, 1, device_id=at_prefix(lax.rem(me + i, NP)), device_id_type=MESH
        )

    @pl.loop(1, NS)
    def _(i):
        pl.semaphore_signal(
            barrier, 1, device_id=at_sample(lax.rem(spos + i, NS)), device_id_type=MESH
        )

    for h in range(HEADS):
        q32[2 * h : 2 * h + 2, :] = q_ref[:, h * 128 : (h + 1) * 128].astype(F32)
    qall[y, z] = q32[...].astype(BF)

    pl.semaphore_wait(barrier, NP - 1 + NS - 1)

    for i in range(1, NZ):
        remote(
            qall.at[y, z],
            qall.at[y, z],
            aq_z.at[0, i],
            aq_z.at[1, z],
            at_zy(lax.rem(z + i, NZ), y),
        ).start()

    @pl.loop(0, 2 * NP)
    def _(r):
        value = sprompt_ref[lax.rem(r, NP) * 16 + 2 * spos + r // NP] - 2 * spos
        row = jnp.full((1, 128), value, jnp.int32).astype(F32)
        sel[pl.ds(r, 1), :] = row
        sel[pl.ds(r + 2 * NP, 1), :] = row

    for j in range(CHUNKS):
        cols = slice(j * 128, (j + 1) * 128)
        resid[2 * j : 2 * j + 2, :] = resid_ref[:, cols].astype(F32)
        gains[0, 2 * j : 2 * j + 2, :] = jnp.broadcast_to(again_ref[:, cols], (2, 128))
        gains[1, 2 * j : 2 * j + 2, :] = jnp.broadcast_to(fgain_ref[:, cols], (2, 128))

    msufx[...] = jnp.full(msufx.shape, NEGATIVE, F32)
    lsufx[...] = jnp.zeros(lsufx.shape, F32)
    osufx[...] = jnp.zeros(osufx.shape, F32)
    first_row = lax.broadcasted_iota(jnp.int32, (16, 2048), 0) == 0
    for s in range(2):
        for t in range(2):
            row = jnp.broadcast_to(fresh_ref[s, t : t + 1, :].astype(F32), (16, 2048))
            skv[s, t, SUF:SUFX, :] = jnp.where(first_row, row, 0.0).astype(BF)
    for s in range(2):
        loads[2 * s].wait()
    for k in range(KV):
        lanes = slice(k * 128, (k + 1) * 128)
        rows = q32[4 * k : 4 * k + 4, :].astype(BF)
        odd = lax.broadcasted_iota(jnp.int32, (4, SUFX), 0) % 2 == 1
        ssuf[4 * k : 4 * k + 4, :] = jnp.where(
            odd, dot_t(rows, skv[1, 0, :, lanes]), dot_t(rows, skv[0, 0, :, lanes])
        )
    odd = lax.broadcasted_iota(jnp.int32, (64, SUFX), 0) % 2 == 1
    slot = lax.broadcasted_iota(jnp.int32, (64, SUFX), 1)
    length = jnp.where(odd, slen_ref[1], slen_ref[0])
    scores = jnp.where((slot < length) | (slot == SUF), ssuf[...] * SCALE, NEGATIVE)
    msuf = jnp.max(scores, axis=1, keepdims=True)
    expo = jnp.exp(scores - msuf)
    lsuf = jnp.broadcast_to(jnp.sum(expo, axis=1, keepdims=True), (64, 128))
    msuf = jnp.broadcast_to(msuf, (64, 128))
    even_w = jnp.where(odd, 0.0, expo)
    odd_w = jnp.where(odd, expo, 0.0)
    for s in range(2):
        loads[2 * s + 1].wait()
    for k in range(KV):
        lanes = slice(k * 128, (k + 1) * 128)
        part = slice(4 * k, 4 * k + 4)
        o = dot(even_w[part].astype(BF), skv[0, 1, :, lanes]) + dot(
            odd_w[part].astype(BF), skv[1, 1, :, lanes]
        )
        for g in range(2):
            for s in range(2):
                src = 4 * k + 2 * g + s
                dst = k * 128 + g * 64 + s * 32 + me
                msufx[pl.ds(dst, 1), :] = msuf[src : src + 1]
                lsufx[pl.ds(dst, 1), :] = lsuf[src : src + 1]
                osufx[pl.ds(dst, 1), :] = o[2 * g + s : 2 * g + s + 1]

    def q_slot(zz):
        return qall.at[y, zz]

    for i in range(1, NZ):
        zz = lax.rem(z + i, NZ)
        remote(q_slot(zz), q_slot(zz), aq_z.at[0, i], aq_z.at[1, zz], at_zy(z, y)).wait_recv()
    for i in Y_OFFSETS:
        remote(
            qall.at[y],
            qall.at[y],
            aq_y.at[0, i],
            aq_y.at[1, y],
            at_zy(z, lax.rem(y + i, NY)),
        ).start()
    for i in range(1, NZ):
        zz = lax.rem(z + i, NZ)
        remote(q_slot(z), q_slot(z), aq_z.at[0, i], aq_z.at[1, zz], at_zy(z, y)).wait_send()

    def widen(yy):
        for zz in range(NZ):
            start = pl.multiple_of((zz * NY + yy) * 64, 64)
            qflat[pl.ds(start, 64), :] = qall[yy, zz].astype(F32)

    widen(y)
    for i in Y_OFFSETS:
        yy = lax.rem(y + i, NY)
        remote(qall.at[yy], qall.at[yy], aq_y.at[0, i], aq_y.at[1, yy], at_zy(z, y)).wait_recv()
        widen(yy)
    for i in Y_OFFSETS:
        remote(qall.at[y], qall.at[y], aq_y.at[0, i], aq_y.at[1, y], at_zy(z, y)).wait_send()

    loads[4].wait()
    chosen = sel[...] > 0.5
    lane = lax.broadcasted_iota(jnp.int32, (128, 128), 1)

    def o_copy(k, g):
        h = 2 * k + g
        return remote(
            osend.at[k, g], orecv.at[me], c_o.at[0, h], c_o.at[1, me], at_prefix(h)
        )

    @pl.loop(0, KV)
    def _(i):
        k = lax.rem(me // 2 + 1 + i, KV)
        lanes = pl.ds(pl.multiple_of(k * 128, 128), 128)
        rows = pl.ds(pl.multiple_of(k * 128, 128), 128)
        q = jnp.concatenate(
            [qflat[pl.ds(4 * k + t, 32, stride=64), :] for t in range(4)], axis=0
        ).astype(BF)
        scores = jnp.where(chosen, dot_t(q, pkv[1, 0, :, lanes]), dot_t(q, pkv[0, 0, :, lanes]))
        scores = scores * SCALE
        ms = msufx[rows, :]
        m = jnp.maximum(ms, jnp.max(scores, axis=1, keepdims=True))
        expo = jnp.exp(scores - m)
        a = jnp.exp(ms - m)
        total = jnp.sum(expo, axis=1, keepdims=True) + a * lsufx[rows, :]
        w0 = jnp.where(chosen, 0.0, expo).astype(BF)
        w1 = jnp.where(chosen, expo, 0.0).astype(BF)
        o = dot(w0, pkv[0, 1, :, lanes]) + dot(w1, pkv[1, 1, :, lanes]) + a * osufx[rows, :]
        o = o.astype(BF)
        stat[...] = jnp.where(lane == k, m, jnp.where(lane == KV + k, total, stat[...]))
        for g in range(2):
            osend[k, g] = o[g * 64 : (g + 1) * 64]

            @pl.when(2 * k + g != me)
            def _():
                o_copy(k, g).start()

            @pl.when(2 * k + g == me)
            def _():
                orecv[me] = o[g * 64 : (g + 1) * 64]

    turned = stat[...].T
    stsend[...] = jnp.zeros(stsend.shape, F32)
    stsend[pl.ds(0, KV, stride=8), :] = turned[0:KV]
    stsend[pl.ds(1, KV, stride=8), :] = turned[KV : 2 * KV]

    def tile(n):
        return pl.ds(pl.multiple_of(n * 8, 8), 8)

    def st_copy(i):
        h = lax.rem(me + i, NP)
        return remote(
            stsend.at[tile(h // 2)],
            strecv.at[tile(me)],
            c_st.at[0, i],
            c_st.at[1, me],
            at_prefix(h),
        )

    @pl.loop(1, NP)
    def _(i):
        st_copy(i).start()

    strecv[tile(me), :] = stsend[tile(me // 2), :]

    @pl.loop(1, NP)
    def _(i):
        src = lax.rem(me + i, NP)
        remote(
            stsend.at[tile(0)], strecv.at[tile(src)], c_st.at[0, i], c_st.at[1, src], at_prefix(me)
        ).wait_recv()
        remote(
            osend.at[0, 0], orecv.at[src], c_o.at[0, src], c_o.at[1, src], at_prefix(me)
        ).wait_recv()

    maxima = strecv[pl.ds(0, NP, stride=8), :]
    totals = strecv[pl.ds(1, NP, stride=8), :]
    second = jnp.zeros((NP, 128), jnp.int32) + lax.rem(me, 2) == 1
    maxima = jnp.where(second, pltpu.roll(maxima, 64, 1), maxima)
    totals = jnp.where(second, pltpu.roll(totals, 64, 1), totals)
    factor = jnp.exp(maxima - jnp.max(maxima, axis=0, keepdims=True))
    share = factor / jnp.sum(factor * totals, axis=0, keepdims=True)
    share = jnp.concatenate([share, jnp.zeros((128 - NP, 128), F32)], axis=0).T[0:64]
    merged = jnp.zeros((64, 128), F32)
    for p in range(NP):
        merged = merged + share[:, p : p + 1] * orecv[p].astype(F32)
    attended = merged.astype(BF)

    loads[5].wait()
    for j in range(CHUNKS // 2):
        r = dot(attended, wout[:, 256 * j : 256 * (j + 1)])
        for t in range(2):
            for s in range(2):
                pf[pl.ds(4 * j + 2 * t + s, NP, stride=PROJ_ROWS), :] = r[
                    s * 32 : (s + 1) * 32, t * 128 : (t + 1) * 128
                ]
    for s in range(2 * CHUNKS, PROJ_ROWS):
        pf[pl.ds(s, NP, stride=PROJ_ROWS), :] = jnp.zeros((NP, 128), F32)

    def narrowed(o):
        return pf[pl.ds(pl.multiple_of(o * PROJ_ROWS, 8), PROJ_ROWS), :].astype(BF)

    def p_copy(i):
        o = lax.rem(me + i, NP)
        return remote(psend.at[o], precv.at[me], d_p.at[0, i], d_p.at[1, me], at_prefix(o))

    @pl.loop(1, NP)
    def _(i):
        o = lax.rem(me + i, NP)
        psend[o] = narrowed(o)
        p_copy(i).start()

    precv[me] = narrowed(me)

    @pl.loop(1, NP)
    def _(i):
        src = lax.rem(me + i, NP)
        remote(
            psend.at[0], precv.at[src], d_p.at[0, i], d_p.at[1, src], at_prefix(me)
        ).wait_recv()

    projected = precv[0].astype(F32)
    for p in range(1, NP):
        projected = projected + precv[p].astype(F32)

    row = lax.broadcasted_iota(jnp.int32, (PROJ_ROWS, 128), 0)
    odd = row % 2 == 1
    real = row < 2 * CHUNKS

    def normed(values, gain):
        square = jnp.where(real, values * values, 0.0)
        second = jnp.sum(jnp.where(odd, square, 0.0))
        first = jnp.sum(jnp.where(odd, 0.0, square))
        inv = jnp.where(odd, second, first) * (1.0 / D) + EPSILON
        return values * lax.rsqrt(inv) * gain

    midway = (resid[...] + normed(projected, gains[0])).astype(BF)
    settled = midway.astype(F32)
    ffn_in = normed(settled, gains[1]).astype(BF).astype(F32)
    ffn_in = jnp.where(real, ffn_in, 0.0)

    lane = lax.broadcasted_iota(jnp.int32, (12, 128), 1)
    rolled = [ffn_in if o == 0 else pltpu.roll(ffn_in, 128 - o, 1) for o in (0, 32, 64, 96)]
    for b in range(NS):
        o, j0 = 32 * (b % 4), (21 * b) // 4
        v = rolled[b % 4]
        piece = v[2 * j0 : 2 * j0 + 12]
        if o:
            piece = jnp.where(lane < 128 - o, piece, v[2 * j0 + 2 : 2 * j0 + 14])
        e1send[b] = jnp.concatenate([piece, jnp.zeros((4, 128), F32)], axis=0).astype(BF)

    def e_copy(i):
        b = lax.rem(spos + i, NS)
        return remote(e1send.at[b], e1recv.at[spos], e_1.at[0, i], e_1.at[1, spos], at_sample(b))

    for i in range(1, NS):
        e_copy(i).start()
    e1recv[spos] = e1send[spos]
    for j in range(CHUNKS):
        mid_ref[:, j * 128 : (j + 1) * 128] = settled[2 * j : 2 * j + 2].astype(BF)
    for i in range(1, NS):
        src = lax.rem(spos + i, NS)
        remote(
            e1send.at[0], e1recv.at[src], e_1.at[0, i], e_1.at[1, src], at_sample(spos)
        ).wait_recv()
    for b in range(NS):
        e1f[16 * b : 16 * (b + 1), :] = e1recv[b].astype(F32)
    for i in range(6):
        for s in range(2):
            xf[i, pl.ds(s, 8, stride=2), :] = e1f[pl.ds(2 * i + s, 8, stride=16), :]
    for i in range(6):
        xall[y, z, :, i * 128 : (i + 1) * 128] = xf[i].astype(BF)

    for i in range(1, NZ):
        remote(
            xall.at[y, z],
            xall.at[y, z],
            e_z.at[0, i],
            e_z.at[1, z],
            at_zy(lax.rem(z + i, NZ), y),
        ).start()
    for i in range(1, NZ):
        zz = lax.rem(z + i, NZ)
        remote(
            xall.at[y, z], xall.at[y, zz], e_z.at[0, i], e_z.at[1, zz], at_zy(z, y)
        ).wait_recv()
    for i in Y_OFFSETS:
        remote(
            xall.at[y], xall.at[y], e_y.at[0, i], e_y.at[1, y], at_zy(z, lax.rem(y + i, NY))
        ).start()

    for n in (6, 7, 8):
        loads[n].wait()
    order = (0,) + Y_OFFSETS
    ending = []

    def in_chunk(ci):
        i = order[ci]
        yy = lax.rem(y + i, NY)
        if i:
            remote(
                xall.at[y], xall.at[yy], e_y.at[0, i], e_y.at[1, yy], at_zy(z, y)
            ).wait_recv()
        v = xall[yy].reshape(128, 768)[:, :BLOCK]
        gu[ci, :, 0] = dot(v, wg[...]).astype(BF).reshape(NZ, 16, BLOCK)
        gu[ci, :, 1] = dot(v, wu[...]).astype(BF).reshape(NZ, 16, BLOCK)
        cp = remote(
            gu.at[ci, pl.ds(4 * (1 - c), 4)],
            gurecv.at[ci],
            f_c.at[0, ci],
            f_c.at[1, ci],
            at_xc(x, 1 - c),
        )
        cp.start()
        return cp

    core_copies = [None] * 4
    hid_copies = [None] * 4
    x_copies = [[] for _ in range(4)]

    def stage_a(ci):
        core_copies[ci] = in_chunk(ci)

    def stage_b(ci):
        core_copies[ci].wait_recv()
        ending.append(core_copies[ci])
        for xx in range(NX):
            xs[ci, xx] = (gu[ci, 4 * c + xx].astype(F32) + gurecv[ci, xx].astype(F32)).astype(BF)
        for i in (1, 3, 2):
            xx = lax.rem(x + i, NX)
            cp = remote(
                xs.at[ci, xx],
                xsrecv.at[ci, i],
                f_x.at[0, ci, i],
                f_x.at[1, ci, i],
                at_xc(xx, c),
            )
            cp.start()
            x_copies[ci].append(cp)

    def stage_c(ci):
        total = xs[ci, x].astype(F32)
        for cp, i in zip(x_copies[ci], (1, 3, 2)):
            cp.wait_recv()
            total = total + xsrecv[ci, i].astype(F32)
        ending.extend(x_copies[ci])
        hidden = (jax.nn.gelu(total[0], approximate=True) * total[1]).astype(BF)
        hid[ci, 4 * c + x] = hidden
        x_copies[ci] = []
        for i in (1, 3, 2):
            cp = remote(
                hid.at[ci, 4 * c + x],
                hid.at[ci, 4 * c + x],
                f_hx.at[0, ci, i],
                f_hx.at[1, ci, x],
                at_xc(lax.rem(x + i, NX), c),
            )
            cp.start()
            ending.append(cp)

    def stage_d(ci):
        for i in (1, 3, 2):
            xx = lax.rem(x + i, NX)
            remote(
                hid.at[ci, 0],
                hid.at[ci, 4 * c + xx],
                f_hx.at[0, ci, i],
                f_hx.at[1, ci, xx],
                at_xc(x, c),
            ).wait_recv()
        half = hid.at[ci, pl.ds(4 * c, 4)]
        cp = remote(half, half, f_hc.at[0, ci], f_hc.at[1, ci], at_xc(x, 1 - c))
        cp.start()
        hid_copies[ci] = cp
        ending.append(cp)

    def stage_e(ci):
        half = hid.at[ci, pl.ds(4 * (1 - c), 4)]
        remote(half, half, f_hc.at[0, ci], f_hc.at[1, ci], at_xc(x, c)).wait_recv()
        i = order[ci]
        ysend[ci] = dot(hid[ci].reshape(128, BLOCK), wd[...]).astype(BF).reshape(NZ, 16, BLOCK)
        if i:
            cp = remote(
                ysend.at[ci],
                yrecv.at[ci],
                g_y.at[0, ci],
                g_y.at[1, ci],
                at_zy(z, lax.rem(y + i, NY)),
            )
            cp.start()
            ending.append(cp)

    stages = (stage_a, stage_b, stage_c, stage_d, stage_e)
    for t in range(4 + 4):
        for st in reversed(range(5)):
            if 0 <= t - st < 4:
                stages[st](t - st)

    for ci in range(1, 4):
        remote(
            ysend.at[ci], yrecv.at[ci], g_y.at[0, ci], g_y.at[1, ci], at_zy(z, y)
        ).wait_recv()
    for zz in range(NZ):
        total = ysend[0, zz].astype(F32)
        for ci in range(1, 4):
            total = total + yrecv[ci, zz].astype(F32)
        zsend[zz] = total.astype(BF)
    for i in range(1, NZ):
        zz = lax.rem(z + i, NZ)
        cp = remote(zsend.at[zz], zrecv.at[i], g_z.at[0, i], g_z.at[1, i], at_zy(zz, y))
        cp.start()
        ending.append(cp)
    total = zsend[z].astype(F32)
    for i in range(1, NZ):
        remote(zsend.at[0], zrecv.at[i], g_z.at[0, i], g_z.at[1, i], at_zy(z, y)).wait_recv()
        total = total + zrecv[i].astype(F32)
    out_ref[...] = total.astype(BF)

    for cp in ending:
        cp.wait_send()

    @pl.loop(0, NP)
    def _(h):
        @pl.when(h != me)
        def _():
            o_copy(h // 2, lax.rem(h, 2)).wait_send()

    @pl.loop(1, NP)
    def _(i):
        st_copy(i).wait_send()
        p_copy(i).wait_send()

    for i in range(1, NS):
        e_copy(i).wait_send()
    for i in range(1, NZ):
        remote(xall.at[y, z], xall.at[y, z], e_z.at[0, i], e_z.at[1, z], at_zy(z, y)).wait_send()
    for i in Y_OFFSETS:
        remote(xall.at[y], xall.at[y], e_y.at[0, i], e_y.at[1, y], at_zy(z, y)).wait_send()


def local(
    residual,
    queries,
    fresh_key_value,
    prompt_key_value,
    suffix_key_value,
    suffix_len,
    sample_prompt,
    out_weight,
    attn_gain,
    ffn_gain,
    gate_weight,
    up_weight,
    down_weight,
):
    vmem = pl.BlockSpec(memory_space=pltpu.VMEM)
    smem = pl.BlockSpec(memory_space=pltpu.SMEM)
    hbm = pl.BlockSpec(memory_space=pl.ANY)
    V = pltpu.VMEM
    dma = pltpu.SemaphoreType.DMA
    scratch = [
        V((2, 2, 128, 2048), BF),
        V((2, 2, SUFX, 2048), BF),
        V((128, D), BF),
        V((BLOCK, BLOCK), BF),
        V((BLOCK, BLOCK), BF),
        V((BLOCK, BLOCK), BF),
        dma((9,)),
        V((64, 128), F32),
        V((NY, NZ, 64, 128), BF),
        V((NP * 64, 128), F32),
        V((128, 128), F32),
        V((64, SUFX), F32),
        V((KV * 128, 128), F32),
        V((KV * 128, 128), F32),
        V((KV * 128, 128), F32),
        V((128, 128), F32),
        V((KV, 2, 64, 128), BF),
        V((NP, 64, 128), BF),
        V((KV * 8, 128), F32),
        V((NP * 8, 128), F32),
        V((NP * PROJ_ROWS, 128), F32),
        V((NP, PROJ_ROWS, 128), BF),
        V((NP, PROJ_ROWS, 128), BF),
        V((2, PROJ_ROWS, 128), F32),
        V((PROJ_ROWS, 128), F32),
        V((NS, 16, 128), BF),
        V((NS, 16, 128), BF),
        V((NS * 16, 128), F32),
        V((6, 16, 128), F32),
        V((NY, NZ, 16, 768), BF),
        V((4, NZ, 2, 16, BLOCK), BF),
        V((4, 4, 2, 16, BLOCK), BF),
        V((4, 4, 2, 16, BLOCK), BF),
        V((4, 4, 2, 16, BLOCK), BF),
        V((4, NZ, 16, BLOCK), BF),
        V((4, NZ, 16, BLOCK), BF),
        V((4, NZ, 16, BLOCK), BF),
        V((NZ, 16, BLOCK), BF),
        V((NZ, 16, BLOCK), BF),
        dma((2, NZ)),
        dma((2, NY)),
        dma((2, NP)),
        dma((2, NP)),
        dma((2, NP)),
        dma((2, NS)),
        dma((2, NZ)),
        dma((2, NY)),
        dma((2, 4)),
        dma((2, 4, 4)),
        dma((2, 4, 4)),
        dma((2, 4)),
        dma((2, 4)),
        dma((2, NZ)),
    ]
    return pl.pallas_call(
        body,
        out_shape=(
            jax.ShapeDtypeStruct((2, D), BF),
            jax.ShapeDtypeStruct((16, BLOCK), BF),
        ),
        in_specs=[vmem] * 5 + [smem] * 2 + [hbm] * 6,
        out_specs=(vmem, vmem),
        scratch_shapes=scratch,
        compiler_params=pltpu.CompilerParams(
            collective_id=0, has_side_effects=True, vmem_limit_bytes=56 << 20
        ),
        name="layer",
    )(
        queries,
        fresh_key_value,
        residual,
        attn_gain.reshape(1, D),
        ffn_gain.reshape(1, D),
        suffix_len,
        sample_prompt,
        prompt_key_value,
        suffix_key_value,
        out_weight,
        gate_weight,
        up_weight,
        down_weight,
    )


def solution(mesh):
    return jax.shard_map(
        local,
        mesh=mesh,
        in_specs=(
            P(("prefix", "sample"), None),
            P(("prefix", "sample"), None),
            P(("prefix", "sample"), None, None),
            P("sample", None, "prefix", None),
            P(("prefix", "sample"), None, None, None),
            P(("prefix", "sample")),
            P(),
            P("prefix", None),
            P(),
            P(),
            P("sample", "prefix"),
            P("sample", "prefix"),
            P("prefix", "sample"),
        ),
        out_specs=(P(("prefix", "sample"), None), P("prefix", "sample")),
        check_vma=False,
    )
```

time: 743 us -> 130 us (0.17)
  waiting for transfers between devices: 583 us -> 0 us
  Pallas kernels: 0 us -> 123 us
  blocking collectives: 42.3 us -> 0 us
  local copies, waits for them, and re-layouts: 47.1 us -> 5.42 us
  starting transfers between devices: 22.6 us -> 0 us
  matrix products: 17.1 us -> 0 us
  between operations: 14.7 us -> 0.64 us
  other arithmetic: 10.1 us -> 0 us
    reduce_scatter x1 -> x0, waiting for transfers between devices: 213 us -> none  [local(): lax.psum_scatter(jnp.dot(hidden, down_weight, preferred_element_type=jnp....]
    unnamed x5 -> x0, waiting for transfers between devices: 157 us -> none
    pallas_call x0 -> x1, Pallas kernels: none -> 123 us  [local(): pl.pallas_call(body, out_shape=(jax.ShapeDtypeStruct((2, D), BF), jax.Sha...]
    all_gather x1 -> x0, waiting for transfers between devices: 120 us -> none  [local(): lax.all_gather(ffn_in, ('prefix', 'sample'), axis=0, tiled=True)]
    psum x1 -> x0, waiting for transfers between devices: 68.1 us -> none  [local(): gate_sum, up_sum = lax.psum((gate_part, up_part), 'sample')]
    all_gather x1 -> x0, blocking collectives: 42.3 us -> none  [local(): queries_by_row = lax.all_gather(queries, 'prefix', axis=0, tiled=True)]
    all_to_all x3 -> x0, waiting for transfers between devices: 25.2 us -> none  [the longest x1 17.4 us: local(): lax.all_to_all(blended[None], 'prefix', split_axis=2, concat_axis=0, tile...]
    all_to_all x3 -> x0, starting transfers between devices: 22.4 us -> none  [the longest x1 13.2 us: local(): lax.all_to_all(row_max[None], 'prefix', split_axis=2, concat_axis=0, tile...]
  transfers between devices with their start and end apart: 7 -> 0, of which waited for: 6 -> 0; matrix products, arithmetic and copies ran while one was open for 2% -> 0% of each run, Pallas kernels for 0% -> 0%
where the time goes in v1:
time: 130 us; the launch traced here: 129 us
  Pallas kernels  123 us (95%)
  local copies, waits for them, and re-layouts  5.42 us (4%)
    pallas_call x1, Pallas kernels, local(): pl.pallas_call(body, out_shape=(jax.ShapeDtypeStruct((2, D), BF), jax.Sha...  123 us
    unnamed x2, local copies, waits for them, and re-layouts  2.7 us

profile of v1, /device:TPU:1, one launch (start us, length us, event | category | flops | bytes accessed | tf_op | source)
XLA Modules:
  0.0 129.3 jit_solution(5850437535968047154)
XLA Ops:
  0.6 1.4 %reshape.10.again_ref = f32[1,5376]{1,0:T(1,128)} reshape(f32[5376]{0:T(1024)} %param.21) | data formatting | bytes 43008 | tf_op jit(solution)/shard_map/reshape | solution.py:699
  2.0 1.4 %reshape.11.fgain_ref = f32[1,5376]{1,0:T(1,128)} reshape(f32[5376]{0:T(1024)} %param.22) | data formatting | bytes 43008 | tf_op jit(solution)/shard_map/reshape | solution.py:700
  3.3 123.3 %layer.1 = (bf16[2,5376]{1,0:T(2,128)(2,1)}, bf16[16,672]{1,0:T(8,128)(2,1)}) custom-call(bf16[2,4096]{1,0:T(2,128)(2,1)} %q_ref.1, bf16[2,2,2048]{2,1,0:T(2,128)(2,1)} %fresh_ref.1, bf16[2,5376]{1,0:T(2,128)(2,1)} %resid_ref.1, f32[1,5376]{1,0:T(1,128)} %reshape.10.again_ref, f32[1,5376]{1,0:T(1,128)} %reshape.11.fgain_ref, s32[2]{0:T(128)} %slen_ref.1, ...), custom_call_target="tpu_custom_call" | custom-call | tf_op jit(solution)/shard_map/layer/pallas_call | solution.py:682
  126.6 1.4 %copy.17 = bf16[2,5376]{1,0:T(2,128)(2,1)} copy(bf16[2,5376]{1,0:T(2,128)(2,1)} %get-tuple-element.4) | data formatting | bytes 43008
  128.0 1.3 %copy.18 = bf16[16,672]{1,0:T(8,128)(2,1)} copy(bf16[16,672]{1,0:T(8,128)(2,1)} %get-tuple-element.5) | data formatting | bytes 43008

commit v2 on v1

v2 whole, which is shorter than its diff:
```python
import functools

import jax
import jax.numpy as jnp
from jax import lax
from jax.experimental import pallas as pl
from jax.experimental.pallas import tpu as pltpu
from jax.sharding import PartitionSpec as P

MESH = pl.DeviceIdType.MESH
SCALE = 168.0 ** (-0.5)
NEGATIVE = -1e30
EPSILON = 1e-06
BF = jnp.bfloat16
F32 = jnp.float32

NZ, NY, NX, NC = 8, 4, 4, 2
NP, NS = NZ * NY, NX * NC
HEADS, KV, WIDTH = 32, 16, 128
D = 5376
CHUNKS = D // 128
PROJ_ROWS = 88
BLOCK = 672
SUF = 192
SUFX = 208
Y_OFFSETS = X_OFFSETS = (1, 3, 2)
LAG = 2
NEAR = (0, 1, 7, 2, 6, 3, 5, 4)
FAR = (4, 5, 3, 6, 2, 7, 1, 0)
SCHEDULE = "a0 a1 b0 a2 b1 a3 b2 c0 b3 c1 d0 c2 d1 e0 c3 d2 e1 f0 d3 e2 f1 e3 f2 f3"


def dot(a, b):
    return jnp.dot(a, b, preferred_element_type=F32)


def dot_t(a, b):
    return lax.dot_general(a, b, (((1,), (1,)), ((), ())), preferred_element_type=F32)


def remote(src, dst, send_sem, recv_sem, device):
    return pltpu.make_async_remote_copy(
        src_ref=src,
        dst_ref=dst,
        send_sem=send_sem,
        recv_sem=recv_sem,
        device_id=device,
        device_id_type=MESH,
    )


def need(loads, n):
    loads[n].wait()


def body(*refs):
    ending, loads = [], []
    layer(ending, loads, *refs)
    for wait in ending:
        wait()


def layer(
    ending,
    loads,
    q_hbm,
    fresh_hbm,
    resid_hbm,
    again_hbm,
    fgain_hbm,
    slen_hbm,
    sprompt_hbm,
    pkv_hbm,
    skv_hbm,
    wout_hbm,
    wg_hbm,
    wu_hbm,
    wd_hbm,
    mid_hbm,
    out_hbm,
    q_ref,
    fresh_ref,
    resid_ref,
    again_ref,
    fgain_ref,
    slen_ref,
    sprompt_ref,
    mid_ref,
    out_ref,
    out_sem,
    pkv,
    skv,
    wout,
    wg,
    wu,
    wd,
    load_sem,
    q32,
    qall,
    qflat,
    sel,
    ssuf,
    msufx,
    lsufx,
    osufx,
    osend,
    orecv,
    stsend,
    strecv,
    ozsend,
    ozrecv,
    stzsend,
    stzrecv,
    pf,
    psend,
    precv,
    pzsend,
    pzrecv,
    gains,
    resid,
    e1send,
    e1recv,
    e1f,
    xf,
    xall,
    gu,
    gurecv,
    xs,
    xsrecv,
    hid,
    ysend,
    yrecv,
    zsend,
    zrecv,
    aq_z,
    aq_y,
    c_o,
    c_st,
    c_oz,
    c_stz,
    d_y,
    d_z,
    e_1,
    e_z,
    e_y,
    f_c,
    f_x,
    f_hx,
    f_hc,
    g_y,
    g_z,
):
    me = lax.axis_index("prefix")
    spos = lax.axis_index("sample")
    z, y = me // NY, me % NY
    x, c = spos // NC, spos % NC

    def send(src, dst, sem, recv, device):
        remote(src, dst, sem.at[0], sem.at[recv], device).start()

    def all_left(ref, sem):
        ending.append(remote(ref, ref, sem.at[0], sem.at[0], at_xc(x, c)).wait_send)

    def landed(ref, sem, recv):
        remote(ref, ref, sem.at[0], sem.at[recv], at_xc(x, c)).wait_recv()

    def at_zy(zz, yy):
        return {"prefix": zz * NY + yy, "sample": spos}

    def at_sample(s):
        return {"prefix": me, "sample": s}

    def at_xc(xx, cc):
        return {"prefix": me, "sample": xx * NC + cc}

    barrier = pltpu.get_barrier_semaphore()

    for i in range(1, NZ):
        pl.semaphore_signal(
            barrier, 1, device_id=at_zy(lax.rem(z + i, NZ), y), device_id_type=MESH
        )
    for i in range(1, NY):
        pl.semaphore_signal(
            barrier, 1, device_id=at_zy(z, lax.rem(y + i, NY)), device_id_type=MESH
        )

    @pl.loop(1, NS)
    def _(i):
        pl.semaphore_signal(
            barrier, 1, device_id=at_sample(lax.rem(spos + i, NS)), device_id_type=MESH
        )

    def load(src, dst):
        cp = pltpu.make_async_copy(src, dst, load_sem.at[len(loads)])
        cp.start()
        loads.append(cp)

    load(q_hbm, q_ref)
    load(sprompt_hbm, sprompt_ref)
    load(slen_hbm, slen_ref)
    load(fresh_hbm, fresh_ref)
    load(resid_hbm, resid_ref)
    load(again_hbm, again_ref)
    load(fgain_hbm, fgain_ref)
    for t in range(2):
        for s in range(2):
            load(skv_hbm.at[s, t], skv.at[s, t, pl.ds(0, SUF)])
    load(pkv_hbm, pkv)

    need(loads, 0)
    for h in range(HEADS):
        q32[2 * h : 2 * h + 2, :] = q_ref[:, h * 128 : (h + 1) * 128].astype(F32)
    qall[0, 0] = q32[...].astype(BF)

    pl.semaphore_wait(barrier, NZ - 1 + NY - 1 + NS - 1)

    def spread(buf, sem_z, sem_y):
        def to_y(n):
            for i in Y_OFFSETS:
                there = at_zy(z, lax.rem(y + i, NY))
                send(buf.at[n, 0], buf.at[n, (-i) % NY], sem_y, 1 + n, there)

        def start():
            for n in range(NZ - 1, 0, -1):
                slot = NEAR.index((-NEAR[n]) % NZ)
                there = at_zy(lax.rem(z + NEAR[n], NZ), y)
                send(buf.at[0, 0], buf.at[slot, 0], sem_z, 1 + slot, there)
            to_y(0)
            all_left(buf.at[pl.ds(1, NZ - 1), 0], sem_z)
            all_left(buf.at[pl.ds(0, NZ), pl.ds(1, NY - 1)], sem_y)

        def pass_on(n):
            landed(buf.at[n, 0], sem_z, 1 + n)
            to_y(n)

        def take(n):
            landed(buf.at[n, pl.ds(1, NY - 1)], sem_y, 1 + n)

        return start, pass_on, take

    q_start, q_pass, q_take = spread(qall, aq_z, aq_y)
    q_start()

    need(loads, 1)
    @pl.loop(0, 2 * NP)
    def _(r):
        value = sprompt_ref[lax.rem(r, NP) * 16 + 2 * spos + r // NP] - 2 * spos
        row = jnp.full((1, 128), value, jnp.int32).astype(F32)
        sel[pl.ds(r, 1), :] = row
        sel[pl.ds(r + 2 * NP, 1), :] = row

    msufx[...] = jnp.full(msufx.shape, NEGATIVE, F32)
    q_pass(1)

    need(loads, 3)
    first_row = lax.broadcasted_iota(jnp.int32, (16, 2048), 0) == 0
    for s in range(2):
        for t in range(2):
            row = jnp.broadcast_to(fresh_ref[s, t : t + 1, :].astype(F32), (16, 2048))
            skv[s, t, SUF:SUFX, :] = jnp.where(first_row, row, 0.0).astype(BF)
    q_pass(2)
    for s in range(2):
        need(loads, 7 + s)

    def suffix_scores(k):
        lanes = slice(k * 128, (k + 1) * 128)
        rows = q32[4 * k : 4 * k + 4, :].astype(BF)
        odd = lax.broadcasted_iota(jnp.int32, (4, SUFX), 0) % 2 == 1
        ssuf[4 * k : 4 * k + 4, :] = jnp.where(
            odd, dot_t(rows, skv[1, 0, :, lanes]), dot_t(rows, skv[0, 0, :, lanes])
        )

    for k in range(KV // 2):
        suffix_scores(k)
    q_pass(3)
    for k in range(KV // 2, KV):
        suffix_scores(k)
    q_pass(4)
    odd = lax.broadcasted_iota(jnp.int32, (64, SUFX), 0) % 2 == 1
    slot = lax.broadcasted_iota(jnp.int32, (64, SUFX), 1)
    need(loads, 2)
    length = jnp.where(odd, slen_ref[1], slen_ref[0])
    scores = jnp.where((slot < length) | (slot == SUF), ssuf[...] * SCALE, NEGATIVE)
    msuf = jnp.max(scores, axis=1, keepdims=True)
    expo = jnp.exp(scores - msuf)
    lsuf = jnp.broadcast_to(jnp.sum(expo, axis=1, keepdims=True), (64, 128))
    msuf = jnp.broadcast_to(msuf, (64, 128))
    even_w = jnp.where(odd, 0.0, expo)
    odd_w = jnp.where(odd, expo, 0.0)
    q_pass(5)
    q_pass(6)
    q_pass(7)
    lsufx[...] = jnp.zeros(lsufx.shape, F32)
    osufx[...] = jnp.zeros(osufx.shape, F32)
    for s in range(2):
        need(loads, 9 + s)
    for k in range(KV):
        lanes = slice(k * 128, (k + 1) * 128)
        part = slice(4 * k, 4 * k + 4)
        o = dot(even_w[part].astype(BF), skv[0, 1, :, lanes]) + dot(
            odd_w[part].astype(BF), skv[1, 1, :, lanes]
        )
        for g in range(2):
            for s in range(2):
                src = 4 * k + 2 * g + s
                dst = k * 128 + g * 64 + s * 32 + me
                msufx[pl.ds(dst, 1), :] = msuf[src : src + 1]
                lsufx[pl.ds(dst, 1), :] = lsuf[src : src + 1]
                osufx[pl.ds(dst, 1), :] = o[2 * g + s : 2 * g + s + 1]

    for n in range(NZ):
        q_take(n)
        for i in range(NY):
            owner = lax.rem(z + NEAR[n], NZ) * NY + lax.rem(y + i, NY)
            qflat[pl.ds(pl.multiple_of(owner * 64, 64), 64), :] = qall[n, i].astype(F32)

    load(wout_hbm, wout)
    load(wg_hbm, wg)
    load(wu_hbm, wu)
    load(wd_hbm, wd)

    need(loads, 11)
    chosen = sel[...] > 0.5
    lane = lax.broadcasted_iota(jnp.int32, (128, 128), 1)
    diagonal = lax.broadcasted_iota(jnp.int32, (64, 64), 0) == lax.broadcasted_iota(
        jnp.int32, (64, 64), 1
    )

    def attend(k):
        lanes = pl.ds(pl.multiple_of(k * 128, 128), 128)
        rows = pl.ds(pl.multiple_of(k * 128, 128), 128)
        q = jnp.concatenate(
            [qflat[pl.ds(4 * k + t, 32, stride=64), :] for t in range(4)], axis=0
        ).astype(BF)
        scores = jnp.where(chosen, dot_t(q, pkv[1, 0, :, lanes]), dot_t(q, pkv[0, 0, :, lanes]))
        scores = scores * SCALE
        ms = msufx[rows, :]
        m = jnp.maximum(ms, jnp.max(scores, axis=1, keepdims=True))
        expo = jnp.exp(scores - m)
        a = jnp.exp(ms - m)
        total = jnp.sum(expo, axis=1, keepdims=True) + a * lsufx[rows, :]
        w0 = jnp.where(chosen, 0.0, expo).astype(BF)
        w1 = jnp.where(chosen, expo, 0.0).astype(BF)
        o = dot(w0, pkv[0, 1, :, lanes]) + dot(w1, pkv[1, 1, :, lanes]) + a * osufx[rows, :]
        return o.astype(BF), m, total

    def o_to_y(n, i):
        yy = lax.rem(y + i, NY)
        send(osend.at[n, yy], orecv.at[n, (-i) % NY], c_o, 1 + n, at_zy(z, yy))
        send(stsend.at[n], strecv.at[n, (-i) % NY], c_st, 1 + n, at_zy(z, yy))

    def blend(weights, parts):
        total = None
        for low in (False, True):
            pieces = []
            for w in weights:
                w = w[:, :64]
                high = w.astype(BF).astype(F32)
                w = w - high if low else high
                pieces.append(jnp.where(diagonal, jnp.broadcast_to(w, (64, 64)), 0.0).astype(BF))
            term = dot(jnp.concatenate(pieces, axis=1), jnp.concatenate(parts, axis=0))
            total = term if total is None else total + term
        return total

    odd_y = jnp.zeros((1, 128), jnp.int32) + lax.rem(y, 2) == 1
    stat_row = 2 * (y // 2)

    def merge(n):
        maxima, totals, parts = [], [], []
        landed(orecv.at[n, pl.ds(1, NY - 1)], c_o, 1 + n)
        landed(strecv.at[n, pl.ds(1, NY - 1)], c_st, 1 + n)
        for i in range(NY):
            if i:
                parts.append(orecv[n, i])
                m = strecv[n, i, pl.ds(stat_row, 1), :]
                total = strecv[n, i, pl.ds(stat_row + 1, 1), :]
            else:
                parts.append(osend[n, y])
                m = stsend[n, pl.ds(stat_row, 1), :]
                total = stsend[n, pl.ds(stat_row + 1, 1), :]
            maxima.append(jnp.where(odd_y, pltpu.roll(m, 64, 1), m))
            totals.append(jnp.where(odd_y, pltpu.roll(total, 64, 1), total))
        top = functools.reduce(jnp.maximum, maxima)
        weights = [jnp.exp(m - top) for m in maxima]
        total = sum(w * t for w, t in zip(weights, totals))
        ozsend[n] = blend(weights, parts).astype(BF)
        first = lax.broadcasted_iota(jnp.int32, (8, 128), 0) == 0
        stzsend[n] = jnp.where(
            first, jnp.broadcast_to(top, (8, 128)), jnp.broadcast_to(total, (8, 128))
        )
        if FAR[n]:
            there = at_zy(lax.rem(z + FAR[n], NZ), y)
            send(ozsend.at[n], ozrecv.at[n], c_oz, 1 + n, there)
            send(stzsend.at[n], stzrecv.at[n], c_stz, 1 + n, there)

    for n in range(NZ):
        zz = lax.rem(z + FAR[n], NZ)
        o0, m0, t0 = attend(2 * zz)
        o1, m1, t1 = attend(2 * zz + 1)
        for g in range(2):
            osend[n, g] = o0[g * 64 : (g + 1) * 64]
            osend[n, 2 + g] = o1[g * 64 : (g + 1) * 64]
        stats = jnp.where(
            lane == 0, m0, jnp.where(lane == 1, t0, jnp.where(lane == 2, m1, t1))
        )
        stsend[n] = stats.T[0:8]
        for i in Y_OFFSETS:
            o_to_y(n, i)
        if n >= LAG:
            merge(n - LAG)
    for n in range(NZ - LAG, NZ):
        merge(n)

    all_left(orecv.at[pl.ds(0, NZ), pl.ds(1, NY - 1)], c_o)
    all_left(strecv.at[pl.ds(0, NZ), pl.ds(1, NY - 1)], c_st)
    all_left(ozrecv.at[pl.ds(0, NZ - 1)], c_oz)
    all_left(stzrecv.at[pl.ds(0, NZ - 1)], c_stz)

    maxima, totals, parts = [], [], []
    for n in range(NZ - 1):
        landed(ozrecv.at[n], c_oz, 1 + n)
        landed(stzrecv.at[n], c_stz, 1 + n)
        maxima.append(stzrecv[n, 0:1, :])
        totals.append(stzrecv[n, 1:2, :])
        parts.append(ozrecv[n])
    maxima.append(stzsend[NZ - 1, 0:1, :])
    totals.append(stzsend[NZ - 1, 1:2, :])
    parts.append(ozsend[NZ - 1])
    top = functools.reduce(jnp.maximum, maxima)
    weights = [jnp.exp(m - top) for m in maxima]
    total = sum(w * t for w, t in zip(weights, totals))
    attended = blend([w / total for w in weights], parts).astype(BF)

    need(loads, 12)
    for j in range(CHUNKS // 2):
        r = dot(attended, wout[:, 256 * j : 256 * (j + 1)])
        for t in range(2):
            for s in range(2):
                pf[pl.ds(4 * j + 2 * t + s, NP, stride=PROJ_ROWS), :] = r[
                    s * 32 : (s + 1) * 32, t * 128 : (t + 1) * 128
                ]
    for s in range(2 * CHUNKS, PROJ_ROWS):
        pf[pl.ds(s, NP, stride=PROJ_ROWS), :] = jnp.zeros((NP, 128), F32)

    def reduced(n_z, y_out, y_in, z_out, z_in, sem_y, sem_z):
        def to_y(n, i):
            there = at_zy(z, lax.rem(y + i, NY))
            send(y_out.at[n, i], y_in.at[n, (-i) % NY], sem_y, 1 + n, there)

        def add_y(n):
            landed(y_in.at[n, pl.ds(1, NY - 1)], sem_y, 1 + n)
            total = y_out[n, 0].astype(F32)
            for i in Y_OFFSETS:
                total = total + y_in[n, i].astype(F32)
            return total

        def to_z(n, total):
            z_out[n] = total.astype(BF)
            there = at_zy(lax.rem(z + n_z[n], NZ), y)
            send(z_out.at[n], z_in.at[n], sem_z, 1 + n, there)

        def add_z(n):
            landed(z_in.at[n], sem_z, 1 + n)
            return z_in[n].astype(F32)

        all_left(y_in.at[pl.ds(0, NZ), pl.ds(1, NY - 1)], sem_y)
        all_left(z_in.at[pl.ds(0, NZ - 1)], sem_z)
        return to_y, add_y, to_z, add_z

    p_to_y, p_add_y, p_to_z, p_add_z = reduced(FAR, psend, precv, pzsend, pzrecv, d_y, d_z)
    for n in range(NZ):
        for i in Y_OFFSETS + (0,):
            o = lax.rem(z + FAR[n], NZ) * NY + lax.rem(y + i, NY)
            start = pl.multiple_of(o * PROJ_ROWS, 8)
            psend[n, i] = pf[pl.ds(start, PROJ_ROWS), :].astype(BF)
            if i:
                p_to_y(n, i)
    for n in (4, 5, 6):
        need(loads, n)
    for j in range(CHUNKS):
        cols = slice(j * 128, (j + 1) * 128)
        resid[2 * j : 2 * j + 2, :] = resid_ref[:, cols].astype(F32)
        gains[0, 2 * j : 2 * j + 2, :] = jnp.broadcast_to(again_ref[cols].reshape(1, 128), (2, 128))
        gains[1, 2 * j : 2 * j + 2, :] = jnp.broadcast_to(fgain_ref[cols].reshape(1, 128), (2, 128))
    for n in range(NZ - 1):
        p_to_z(n, p_add_y(n))
    projected = p_add_y(NZ - 1)
    for n in range(NZ - 1):
        projected = projected + p_add_z(n)

    row = lax.broadcasted_iota(jnp.int32, (PROJ_ROWS, 128), 0)
    odd = row % 2 == 1
    real = row < 2 * CHUNKS

    def normed(values, gain):
        square = jnp.where(real, values * values, 0.0)
        second = jnp.sum(jnp.where(odd, square, 0.0))
        first = jnp.sum(jnp.where(odd, 0.0, square))
        inv = jnp.where(odd, second, first) * (1.0 / D) + EPSILON
        return values * lax.rsqrt(inv) * gain

    midway = (resid[...] + normed(projected, gains[0])).astype(BF)
    settled = midway.astype(F32)
    ffn_in = normed(settled, gains[1]).astype(BF).astype(F32)
    ffn_in = jnp.where(real, ffn_in, 0.0)

    lane = lax.broadcasted_iota(jnp.int32, (12, 128), 1)
    rolled = [ffn_in if o == 0 else pltpu.roll(ffn_in, 128 - o, 1) for o in (0, 32, 64, 96)]
    for b in range(NS):
        o, j0 = 32 * (b % 4), (21 * b) // 4
        v = rolled[b % 4]
        piece = v[2 * j0 : 2 * j0 + 12]
        if o:
            piece = jnp.where(lane < 128 - o, piece, v[2 * j0 + 2 : 2 * j0 + 14])
        e1send[b] = jnp.concatenate([piece, jnp.zeros((4, 128), F32)], axis=0).astype(BF)

    for i in range(1, NS):
        b = lax.rem(spos + i, NS)
        send(e1send.at[b], e1recv.at[spos], e_1, 1, at_sample(b))
    all_left(e1send.at[pl.ds(1, NS - 1)], e_1)
    e1recv[spos] = e1send[spos]
    for j in range(CHUNKS):
        mid_ref[:, j * 128 : (j + 1) * 128] = settled[2 * j : 2 * j + 2].astype(BF)
    mid_copy = pltpu.make_async_copy(mid_ref, mid_hbm, out_sem.at[0])
    mid_copy.start()
    ending.append(mid_copy.wait)
    landed(e1recv.at[pl.ds(1, NS - 1)], e_1, 1)
    for b in range(NS):
        e1f[16 * b : 16 * (b + 1), :] = e1recv[b].astype(F32)
    for i in range(6):
        for s in range(2):
            xf[i, pl.ds(s, 8, stride=2), :] = e1f[pl.ds(2 * i + s, 8, stride=16), :]
    for i in range(6):
        xall[0, 0, :, i * 128 : (i + 1) * 128] = xf[i].astype(BF)

    x_start, x_pass, x_take = spread(xall, e_z, e_y)
    x_start()
    for n in (13, 14, 15):
        need(loads, n)

    def stage_a(ci):
        for n in (2 * ci, 2 * ci + 1):
            x_take(n)
        v = xall[2 * ci : 2 * ci + 2].reshape(128, 768)[:, :BLOCK]
        gu[ci, :, 0] = dot(v, wg[...]).astype(BF).reshape(NZ, 16, BLOCK)
        gu[ci, :, 1] = dot(v, wu[...]).astype(BF).reshape(NZ, 16, BLOCK)
        send(gu.at[ci, pl.ds(4 * (1 - c), 4)], gurecv.at[ci], f_c, 1 + ci, at_xc(x, 1 - c))

    def stage_b(ci):
        landed(gurecv.at[ci], f_c, 1 + ci)
        for xx in range(NX):
            xs[ci, xx] = (gu[ci, 4 * c + xx].astype(F32) + gurecv[ci, xx].astype(F32)).astype(BF)
        for i in X_OFFSETS:
            xx = lax.rem(x + i, NX)
            send(xs.at[ci, xx], xsrecv.at[ci, i], f_x, 1 + ci, at_xc(xx, c))

    def stage_c(ci):
        landed(xsrecv.at[ci, pl.ds(1, NX - 1)], f_x, 1 + ci)
        total = xs[ci, x].astype(F32)
        for i in X_OFFSETS:
            total = total + xsrecv[ci, i].astype(F32)
        own = hid.at[ci, 4 * c + x]
        own[...] = (jax.nn.gelu(total[0], approximate=True) * total[1]).astype(BF)
        for i in X_OFFSETS:
            send(own, own, f_hx, 1 + ci, at_xc(lax.rem(x + i, NX), c))

    def stage_d(ci):
        landed(hid.at[ci, pl.ds(0, NX - 1)], f_hx, 1 + ci)
        half = hid.at[ci, pl.ds(4 * c, 4)]
        send(half, half, f_hc, 1 + ci, at_xc(x, 1 - c))

    all_left(gurecv, f_c)
    all_left(xsrecv.at[pl.ds(0, 4), pl.ds(1, NX - 1)], f_x)
    all_left(hid.at[pl.ds(0, 4), pl.ds(0, NX - 1)], f_hx)
    all_left(hid.at[pl.ds(0, 4), pl.ds(0, 4)], f_hc)
    y_to_y, y_add_y, y_to_z, y_add_z = reduced(NEAR, ysend, yrecv, zsend, zrecv, g_y, g_z)

    def stage_e(ci):
        landed(hid.at[ci, pl.ds(4 * (1 - c), 4)], f_hc, 1 + ci)
        two = dot(hid[ci].reshape(128, BLOCK), wd[...]).astype(BF).reshape(2, NY, 16, BLOCK)
        ysend[2 * ci : 2 * ci + 2] = two
        for n in (2 * ci, 2 * ci + 1):
            for i in Y_OFFSETS:
                y_to_y(n, i)

    def stage_f(ci):
        for n in (2 * ci, 2 * ci + 1):
            if n:
                y_to_z(n, y_add_y(n))

    for n in range(1, NZ):
        x_pass(n)
    stages = {"a": stage_a, "b": stage_b, "c": stage_c, "d": stage_d, "e": stage_e, "f": stage_f}
    for name in SCHEDULE.split():
        stages[name[0]](int(name[1]))
    total = y_add_y(0)
    for n in range(1, NZ):
        total = total + y_add_z(n)
    out_ref[...] = total.astype(BF)
    out_copy = pltpu.make_async_copy(out_ref, out_hbm, out_sem.at[1])
    out_copy.start()
    ending.append(out_copy.wait)


def local(
    residual,
    queries,
    fresh_key_value,
    prompt_key_value,
    suffix_key_value,
    suffix_len,
    sample_prompt,
    out_weight,
    attn_gain,
    ffn_gain,
    gate_weight,
    up_weight,
    down_weight,
):
    hbm = pl.BlockSpec(memory_space=pl.ANY)
    V = pltpu.VMEM
    dma = pltpu.SemaphoreType.DMA
    scratch = [
        V((2, HEADS * WIDTH), BF),
        V((2, 2, KV * WIDTH), BF),
        V((2, D), BF),
        V((D,), F32),
        V((D,), F32),
        pltpu.SMEM((2,), jnp.int32),
        pltpu.SMEM((2 * NP * NS,), jnp.int32),
        V((2, D), BF),
        V((16, BLOCK), BF),
        dma((2,)),
        V((2, 2, 128, 2048), BF),
        V((2, 2, SUFX, 2048), BF),
        V((128, D), BF),
        V((BLOCK, BLOCK), BF),
        V((BLOCK, BLOCK), BF),
        V((BLOCK, BLOCK), BF),
        dma((16,)),
        V((64, 128), F32),
        V((NZ, NY, 64, 128), BF),
        V((NP * 64, 128), F32),
        V((128, 128), F32),
        V((64, SUFX), F32),
        V((KV * 128, 128), F32),
        V((KV * 128, 128), F32),
        V((KV * 128, 128), F32),
        V((NZ, NY, 64, 128), BF),
        V((NZ, NY, 64, 128), BF),
        V((NZ, 8, 128), F32),
        V((NZ, NY, 8, 128), F32),
        V((NZ, 64, 128), BF),
        V((NZ, 64, 128), BF),
        V((NZ, 8, 128), F32),
        V((NZ, 8, 128), F32),
        V((NP * PROJ_ROWS, 128), F32),
        V((NZ, NY, PROJ_ROWS, 128), BF),
        V((NZ, NY, PROJ_ROWS, 128), BF),
        V((NZ, PROJ_ROWS, 128), BF),
        V((NZ, PROJ_ROWS, 128), BF),
        V((2, PROJ_ROWS, 128), F32),
        V((PROJ_ROWS, 128), F32),
        V((NS, 16, 128), BF),
        V((NS, 16, 128), BF),
        V((NS * 16, 128), F32),
        V((6, 16, 128), F32),
        V((NZ, NY, 16, 768), BF),
        V((4, NZ, 2, 16, BLOCK), BF),
        V((4, 4, 2, 16, BLOCK), BF),
        V((4, 4, 2, 16, BLOCK), BF),
        V((4, 4, 2, 16, BLOCK), BF),
        V((4, NZ, 16, BLOCK), BF),
        V((NZ, NY, 16, BLOCK), BF),
        V((NZ, NY, 16, BLOCK), BF),
        V((NZ, 16, BLOCK), BF),
        V((NZ, 16, BLOCK), BF),
        dma((1 + NZ,)),
        dma((1 + NZ,)),
        dma((1 + NZ,)),
        dma((1 + NZ,)),
        dma((1 + NZ,)),
        dma((1 + NZ,)),
        dma((1 + NZ,)),
        dma((1 + NZ,)),
        dma((2,)),
        dma((1 + NZ,)),
        dma((1 + NZ,)),
        dma((5,)),
        dma((5,)),
        dma((5,)),
        dma((5,)),
        dma((1 + NZ,)),
        dma((1 + NZ,)),
    ]
    return pl.pallas_call(
        body,
        out_shape=(
            jax.ShapeDtypeStruct((2, D), BF),
            jax.ShapeDtypeStruct((16, BLOCK), BF),
        ),
        in_specs=[hbm] * 13,
        out_specs=(hbm, hbm),
        scratch_shapes=scratch,
        compiler_params=pltpu.CompilerParams(
            collective_id=0, has_side_effects=True, vmem_limit_bytes=56 << 20
        ),
        name="layer",
    )(
        queries,
        fresh_key_value,
        residual,
        attn_gain,
        ffn_gain,
        suffix_len,
        sample_prompt,
        prompt_key_value,
        suffix_key_value,
        out_weight,
        gate_weight,
        up_weight,
        down_weight,
    )


def solution(mesh):
    return jax.shard_map(
        local,
        mesh=mesh,
        in_specs=(
            P(("prefix", "sample"), None),
            P(("prefix", "sample"), None),
            P(("prefix", "sample"), None, None),
            P("sample", None, "prefix", None),
            P(("prefix", "sample"), None, None, None),
            P(("prefix", "sample")),
            P(),
            P("prefix", None),
            P(),
            P(),
            P("sample", "prefix"),
            P("sample", "prefix"),
            P("prefix", "sample"),
        ),
        out_specs=(P(("prefix", "sample"), None), P("prefix", "sample")),
        check_vma=False,
    )
```

time: 130 us -> 100 us (0.77)
  Pallas kernels: 123 us -> 96.8 us
  local copies, waits for them, and re-layouts: 5.42 us -> 2.7 us
    pallas_call x1, Pallas kernels: 123 us -> 96.8 us  [local(): pl.pallas_call(body, out_shape=(jax.ShapeDtypeStruct((2, D), BF), jax.Sha...]
    reshape x2 -> x0, local copies, waits for them, and re-layouts: 2.72 us -> none  [the longest x1 1.36 us: local(): attn_gain.reshape(1, D)]
where the time goes in v2:
time: 100 us
  Pallas kernels  96.8 us (97%)
  local copies, waits for them, and re-layouts  2.7 us (3%)
    pallas_call x1, Pallas kernels, local(): pl.pallas_call(body, out_shape=(jax.ShapeDtypeStruct((2, D), BF), jax.Sha...  96.8 us
    unnamed x2, local copies, waits for them, and re-layouts  2.7 us

profile of v2, /device:TPU:1, one launch (start us, length us, event | category | flops | bytes accessed | tf_op | source)
XLA Modules:
  0.0 100.1 jit_solution(4008568280147985309)
XLA Ops:
  0.6 96.8 %layer.1 = (bf16[2,5376]{1,0:T(2,128)(2,1)}, bf16[16,672]{1,0:T(8,128)(2,1)}) custom-call(bf16[2,4096]{1,0:T(2,128)(2,1)} %refs_0_.1, bf16[2,2,2048]{2,1,0:T(2,128)(2,1)} %refs_1_.1, bf16[2,5376]{1,0:T(2,128)(2,1)} %refs_2_.1, f32[5376]{0:T(1024)} %refs_3_.1, f32[5376]{0:T(1024)} %refs_4_.1, s32[2]{0:T(128)} %refs_5_.1, s32[512]{0:T(512)} %refs_6_.1, ...), custom_call_target="tpu_custom_call" | custom-call | tf_op jit(solution)/shard_map/layer/pallas_call | solution.py:696
  97.4 1.4 %copy.17 = bf16[2,5376]{1,0:T(2,128)(2,1)} copy(bf16[2,5376]{1,0:T(2,128)(2,1)} %get-tuple-element.4) | data formatting | bytes 43008
  98.8 1.3 %copy.18 = bf16[16,672]{1,0:T(8,128)(2,1)} copy(bf16[16,672]{1,0:T(8,128)(2,1)} %get-tuple-element.5) | data formatting | bytes 43008

commit v3 on v2

--- a/solution.py
+++ b/solution.py
@@ -24,10 +24,17 @@
 SUF = 192
 SUFX = 208
 Y_OFFSETS = X_OFFSETS = (1, 3, 2)
-LAG = 2
+LAG = 6
 NEAR = (0, 1, 7, 2, 6, 3, 5, 4)
+FFN_ORDER = (0, 4, 2, 3, 6, 5, 1, 7)
 FAR = (4, 5, 3, 6, 2, 7, 1, 0)
-SCHEDULE = "a0 a1 b0 a2 b1 a3 b2 c0 b3 c1 d0 c2 d1 e0 c3 d2 e1 f0 d3 e2 f1 e3 f2 f3"
+TURNS = 4
+SCHEDULE = (
+    ("a", 0), ("a", 1), ("a", 2), ("a", 3),
+    ("c", 0), ("c", 1), ("c", 2), ("c", 3),
+    ("e", 0), ("e", 1), ("e", 2), ("e", 3),
+    ("f", 0), ("f", 1), ("f", 2), ("f", 3),
+)
 
 
 def dot(a, b):
@@ -91,9 +98,7 @@
     pkv,
     skv,
     wout,
-    wg,
-    wu,
-    wd,
+    ffw,
     load_sem,
     q32,
     qall,
@@ -122,16 +127,16 @@
     e1recv,
     e1f,
     xf,
+    xown,
     xall,
     gu,
     gurecv,
-    xs,
-    xsrecv,
     hid,
     ysend,
     yrecv,
     zsend,
     zrecv,
+    w_c,
     aq_z,
     aq_y,
     c_o,
@@ -143,10 +148,8 @@
     e_1,
     e_z,
     e_y,
-    f_c,
     f_x,
     f_hx,
-    f_hc,
     g_y,
     g_z,
 ):
@@ -167,6 +170,9 @@
     def at_zy(zz, yy):
         return {"prefix": zz * NY + yy, "sample": spos}
 
+    def at_zyc(zz, yy, cc):
+        return {"prefix": zz * NY + yy, "sample": x * NC + cc}
+
     def at_sample(s):
         return {"prefix": me, "sample": s}
 
@@ -176,9 +182,9 @@
     barrier = pltpu.get_barrier_semaphore()
 
     for i in range(1, NZ):
-        pl.semaphore_signal(
-            barrier, 1, device_id=at_zy(lax.rem(z + i, NZ), y), device_id_type=MESH
-        )
+        for cc in range(NC):
+            there = at_zyc(lax.rem(z + i, NZ), y, cc)
+            pl.semaphore_signal(barrier, 1, device_id=there, device_id_type=MESH)
     for i in range(1, NY):
         pl.semaphore_signal(
             barrier, 1, device_id=at_zy(z, lax.rem(y + i, NY)), device_id_type=MESH
@@ -212,9 +218,9 @@
         q32[2 * h : 2 * h + 2, :] = q_ref[:, h * 128 : (h + 1) * 128].astype(F32)
     qall[0, 0] = q32[...].astype(BF)
 
-    pl.semaphore_wait(barrier, NZ - 1 + NY - 1 + NS - 1)
-
-    def spread(buf, sem_z, sem_y):
+    pl.semaphore_wait(barrier, NC * (NZ - 1) + NY - 1 + NS - 1)
+
+    def spread(order, buf, sem_z, sem_y):
         def to_y(n):
             for i in Y_OFFSETS:
                 there = at_zy(z, lax.rem(y + i, NY))
@@ -222,8 +228,8 @@
 
         def start():
             for n in range(NZ - 1, 0, -1):
-                slot = NEAR.index((-NEAR[n]) % NZ)
-                there = at_zy(lax.rem(z + NEAR[n], NZ), y)
+                slot = order.index((-order[n]) % NZ)
+                there = at_zy(lax.rem(z + order[n], NZ), y)
                 send(buf.at[0, 0], buf.at[slot, 0], sem_z, 1 + slot, there)
             to_y(0)
             all_left(buf.at[pl.ds(1, NZ - 1), 0], sem_z)
@@ -238,7 +244,7 @@
 
         return start, pass_on, take
 
-    q_start, q_pass, q_take = spread(qall, aq_z, aq_y)
+    q_start, q_pass, q_take = spread(NEAR, qall, aq_z, aq_y)
     q_start()
 
     need(loads, 1)
@@ -315,9 +321,10 @@
             qflat[pl.ds(pl.multiple_of(owner * 64, 64), 64), :] = qall[n, i].astype(F32)
 
     load(wout_hbm, wout)
-    load(wg_hbm, wg)
-    load(wu_hbm, wu)
-    load(wd_hbm, wd)
+    for t, ref in enumerate((wg_hbm, wu_hbm, wd_hbm)):
+        load(ref, ffw.at[t, c])
+        send(ref, ffw.at[t, c], w_c, 1 + t, at_xc(x, 1 - c))
+    all_left(ffw.at[pl.ds(0, 3), 0], w_c)
 
     need(loads, 11)
     chosen = sel[...] > 0.5
@@ -512,90 +519,142 @@
         piece = v[2 * j0 : 2 * j0 + 12]
         if o:
             piece = jnp.where(lane < 128 - o, piece, v[2 * j0 + 2 : 2 * j0 + 14])
-        e1send[b] = jnp.concatenate([piece, jnp.zeros((4, 128), F32)], axis=0).astype(BF)
+        piece = jnp.concatenate([piece, jnp.zeros((4, 128), F32)], axis=0)
+        e1send[b // NC, b % NC] = piece.astype(BF)
 
     for i in range(1, NS):
         b = lax.rem(spos + i, NS)
-        send(e1send.at[b], e1recv.at[spos], e_1, 1, at_sample(b))
-    all_left(e1send.at[pl.ds(1, NS - 1)], e_1)
-    e1recv[spos] = e1send[spos]
+        send(e1send.at[b // NC], e1recv.at[spos], e_1, 1, at_sample(b))
+    all_left(e1recv.at[pl.ds(1, NS - 1)], e_1)
+    e1recv[spos] = e1send[x]
     for j in range(CHUNKS):
         mid_ref[:, j * 128 : (j + 1) * 128] = settled[2 * j : 2 * j + 2].astype(BF)
     mid_copy = pltpu.make_async_copy(mid_ref, mid_hbm, out_sem.at[0])
     mid_copy.start()
     ending.append(mid_copy.wait)
     landed(e1recv.at[pl.ds(1, NS - 1)], e_1, 1)
-    for b in range(NS):
-        e1f[16 * b : 16 * (b + 1), :] = e1recv[b].astype(F32)
-    for i in range(6):
-        for s in range(2):
-            xf[i, pl.ds(s, 8, stride=2), :] = e1f[pl.ds(2 * i + s, 8, stride=16), :]
-    for i in range(6):
-        xall[0, 0, :, i * 128 : (i + 1) * 128] = xf[i].astype(BF)
-
-    x_start, x_pass, x_take = spread(xall, e_z, e_y)
-    x_start()
-    for n in (13, 14, 15):
-        need(loads, n)
-
-    def stage_a(ci):
-        for n in (2 * ci, 2 * ci + 1):
-            x_take(n)
-        v = xall[2 * ci : 2 * ci + 2].reshape(128, 768)[:, :BLOCK]
-        gu[ci, :, 0] = dot(v, wg[...]).astype(BF).reshape(NZ, 16, BLOCK)
-        gu[ci, :, 1] = dot(v, wu[...]).astype(BF).reshape(NZ, 16, BLOCK)
-        send(gu.at[ci, pl.ds(4 * (1 - c), 4)], gurecv.at[ci], f_c, 1 + ci, at_xc(x, 1 - c))
-
-    def stage_b(ci):
-        landed(gurecv.at[ci], f_c, 1 + ci)
-        for xx in range(NX):
-            xs[ci, xx] = (gu[ci, 4 * c + xx].astype(F32) + gurecv[ci, xx].astype(F32)).astype(BF)
+    for cc in range(NC):
+        for b in range(NS):
+            e1f[16 * b : 16 * (b + 1), :] = e1recv[b, cc].astype(F32)
+        for i in range(6):
+            for s in range(2):
+                xf[i, pl.ds(s, 8, stride=2), :] = e1f[pl.ds(2 * i + s, 8, stride=16), :]
+        for i in range(6):
+            xown[cc, :, i * 128 : (i + 1) * 128] = xf[i].astype(BF)
+
+    def turn(t):
+        return FFN_ORDER[2 * t] * (1 - c) + FFN_ORDER[2 * t + 1] * c
+
+    def x_to_z(t):
+        send(xown, xall.at[t, 0], e_z, 1 + t, at_zy(lax.rem(z + NZ - turn(t), NZ), y))
+
+    def x_to_y(t):
+        for i in Y_OFFSETS:
+            there = at_zy(z, lax.rem(y + i, NY))
+            send(xall.at[t, 0], xall.at[t, (-i) % NY], e_y, 1 + t, there)
+
+    for t in (3, 2, 1):
+        x_to_z(t)
+
+    @pl.when(c == 0)
+    def _():
+        xall[0, 0] = xown[...]
+
+    @pl.when(c == 1)
+    def _():
+        x_to_z(0)
+        landed(xall.at[0, 0], e_z, 1)
+
+    x_to_y(0)
+    for t in range(1, TURNS):
+        landed(xall.at[t, 0], e_z, 1 + t)
+        x_to_y(t)
+    all_left(xall.at[pl.ds(0, TURNS), pl.ds(1, NY - 1)], e_y)
+
+    def some_left(ref, sem):
+        less = ref.at[pl.ds(1, ref.shape[0] - 1)]
+        for cc, sent in ((0, less), (1, ref)):
+
+            @pl.when(c == cc)
+            def _(sent=sent):
+                remote(sent, sent, sem.at[0], sem.at[0], at_xc(x, c)).wait_send()
+
+    ending.append(lambda: some_left(xall.at[pl.ds(0, TURNS), 0], e_z))
+
+    for t in range(3):
+        need(loads, 13 + t)
+        landed(ffw.at[t, 1 - c], w_c, 1 + t)
+
+    def stage_a(t):
+        landed(xall.at[t, pl.ds(1, NY - 1)], e_y, 1 + t)
+        v = [xall[t, :, cc].reshape(64, 768)[:, :BLOCK] for cc in range(NC)]
+        for n in range(2):
+            part = dot(v[0], ffw[n, 0]) + dot(v[1], ffw[n, 1])
+            gu[t, :, n] = part.astype(BF).reshape(NY, 16, BLOCK)
         for i in X_OFFSETS:
             xx = lax.rem(x + i, NX)
-            send(xs.at[ci, xx], xsrecv.at[ci, i], f_x, 1 + ci, at_xc(xx, c))
-
-    def stage_c(ci):
-        landed(xsrecv.at[ci, pl.ds(1, NX - 1)], f_x, 1 + ci)
-        total = xs[ci, x].astype(F32)
+            send(gu.at[t, xx], gurecv.at[t, i], f_x, 1 + t, at_xc(xx, c))
+
+    def stage_c(t):
+        landed(gurecv.at[t, pl.ds(1, NX - 1)], f_x, 1 + t)
+        total = gu[t, x].astype(F32)
         for i in X_OFFSETS:
-            total = total + xsrecv[ci, i].astype(F32)
-        own = hid.at[ci, 4 * c + x]
+            total = total + gurecv[t, i].astype(F32)
+        own = hid.at[t, x]
         own[...] = (jax.nn.gelu(total[0], approximate=True) * total[1]).astype(BF)
         for i in X_OFFSETS:
-            send(own, own, f_hx, 1 + ci, at_xc(lax.rem(x + i, NX), c))
-
-    def stage_d(ci):
-        landed(hid.at[ci, pl.ds(0, NX - 1)], f_hx, 1 + ci)
-        half = hid.at[ci, pl.ds(4 * c, 4)]
-        send(half, half, f_hc, 1 + ci, at_xc(x, 1 - c))
-
-    all_left(gurecv, f_c)
-    all_left(xsrecv.at[pl.ds(0, 4), pl.ds(1, NX - 1)], f_x)
-    all_left(hid.at[pl.ds(0, 4), pl.ds(0, NX - 1)], f_hx)
-    all_left(hid.at[pl.ds(0, 4), pl.ds(0, 4)], f_hc)
-    y_to_y, y_add_y, y_to_z, y_add_z = reduced(NEAR, ysend, yrecv, zsend, zrecv, g_y, g_z)
-
-    def stage_e(ci):
-        landed(hid.at[ci, pl.ds(4 * (1 - c), 4)], f_hc, 1 + ci)
-        two = dot(hid[ci].reshape(128, BLOCK), wd[...]).astype(BF).reshape(2, NY, 16, BLOCK)
-        ysend[2 * ci : 2 * ci + 2] = two
-        for n in (2 * ci, 2 * ci + 1):
-            for i in Y_OFFSETS:
-                y_to_y(n, i)
-
-    def stage_f(ci):
-        for n in (2 * ci, 2 * ci + 1):
-            if n:
-                y_to_z(n, y_add_y(n))
-
+            send(own, own, f_hx, 1 + t, at_xc(lax.rem(x + i, NX), c))
+
+    def stage_e(t):
+        landed(hid.at[t, pl.ds(0, NX - 1)], f_hx, 1 + t)
+        hidden = hid[t].reshape(64, BLOCK)
+        for cc in range(NC):
+            ysend[t, :, cc] = dot(hidden, ffw[2, cc]).astype(BF).reshape(NY, 16, BLOCK)
+        for i in Y_OFFSETS:
+            there = at_zy(z, lax.rem(y + i, NY))
+            send(ysend.at[t, i], yrecv.at[t, (-i) % NY], g_y, 1 + t, there)
+
+    def stage_f(t):
+        landed(yrecv.at[t, pl.ds(1, NY - 1)], g_y, 1 + t)
+        total = ysend[t, 0].astype(F32)
+        for i in Y_OFFSETS:
+            total = total + yrecv[t, i].astype(F32)
+        zsend[t] = total.astype(BF)
+        zz = lax.rem(z + turn(t), NZ)
+        n = 2 * t + c
+
+        def to_core(cc):
+            send(zsend.at[t, cc], zrecv.at[n], g_z, 1 + n, at_zyc(zz, y, cc))
+
+        to_core(1)
+        if t:
+            to_core(0)
+        else:
+
+            @pl.when(c == 1)
+            def _():
+                to_core(0)
+
+    all_left(gurecv.at[pl.ds(0, TURNS), pl.ds(1, NX - 1)], f_x)
+    all_left(hid.at[pl.ds(0, TURNS), pl.ds(0, NX - 1)], f_hx)
+    all_left(yrecv.at[pl.ds(0, TURNS), pl.ds(1, NY - 1)], g_y)
+    ending.append(lambda: some_left(zrecv, g_z))
+    stages = {"a": stage_a, "c": stage_c, "e": stage_e, "f": stage_f}
+    for name, t in SCHEDULE:
+        stages[name](t)
+
+    @pl.when(c == 0)
+    def _():
+        zrecv[0] = zsend[0, 0]
+
+    @pl.when(c == 1)
+    def _():
+        landed(zrecv.at[0], g_z, 1)
+
+    total = zrecv[0].astype(F32)
     for n in range(1, NZ):
-        x_pass(n)
-    stages = {"a": stage_a, "b": stage_b, "c": stage_c, "d": stage_d, "e": stage_e, "f": stage_f}
-    for name in SCHEDULE.split():
-        stages[name[0]](int(name[1]))
-    total = y_add_y(0)
-    for n in range(1, NZ):
-        total = total + y_add_z(n)
+        landed(zrecv.at[n], g_z, 1 + n)
+        total = total + zrecv[n].astype(F32)
     out_ref[...] = total.astype(BF)
     out_copy = pltpu.make_async_copy(out_ref, out_hbm, out_sem.at[1])
     out_copy.start()
@@ -618,6 +677,7 @@
     down_weight,
 ):
     hbm = pl.BlockSpec(memory_space=pl.ANY)
+    vmem = pl.BlockSpec(memory_space=pltpu.VMEM)
     V = pltpu.VMEM
     dma = pltpu.SemaphoreType.DMA
     scratch = [
@@ -634,9 +694,7 @@
         V((2, 2, 128, 2048), BF),
         V((2, 2, SUFX, 2048), BF),
         V((128, D), BF),
-        V((BLOCK, BLOCK), BF),
-        V((BLOCK, BLOCK), BF),
-        V((BLOCK, BLOCK), BF),
+        V((3, NC, BLOCK, BLOCK), BF),
         dma((16,)),
         V((64, 128), F32),
         V((NZ, NY, 64, 128), BF),
@@ -661,20 +719,20 @@
         V((NZ, PROJ_ROWS, 128), BF),
         V((2, PROJ_ROWS, 128), F32),
         V((PROJ_ROWS, 128), F32),
-        V((NS, 16, 128), BF),
-        V((NS, 16, 128), BF),
+        V((NX, NC, 16, 128), BF),
+        V((NS, NC, 16, 128), BF),
         V((NS * 16, 128), F32),
         V((6, 16, 128), F32),
-        V((NZ, NY, 16, 768), BF),
-        V((4, NZ, 2, 16, BLOCK), BF),
-        V((4, 4, 2, 16, BLOCK), BF),
-        V((4, 4, 2, 16, BLOCK), BF),
-        V((4, 4, 2, 16, BLOCK), BF),
-        V((4, NZ, 16, BLOCK), BF),
-        V((NZ, NY, 16, BLOCK), BF),
-        V((NZ, NY, 16, BLOCK), BF),
+        V((NC, 16, 768), BF),
+        V((TURNS, NY, NC, 16, 768), BF),
+        V((TURNS, NX, 2, 16, BLOCK), BF),
+        V((TURNS, NX, 2, 16, BLOCK), BF),
+        V((TURNS, NX, 16, BLOCK), BF),
+        V((TURNS, NY, NC, 16, BLOCK), BF),
+        V((TURNS, NY, NC, 16, BLOCK), BF),
+        V((TURNS, NC, 16, BLOCK), BF),
         V((NZ, 16, BLOCK), BF),
-        V((NZ, 16, BLOCK), BF),
+        dma((4,)),
         dma((1 + NZ,)),
         dma((1 + NZ,)),
         dma((1 + NZ,)),
@@ -684,16 +742,14 @@
         dma((1 + NZ,)),
         dma((1 + NZ,)),
         dma((2,)),
-        dma((1 + NZ,)),
-        dma((1 + NZ,)),
-        dma((5,)),
-        dma((5,)),
-        dma((5,)),
-        dma((5,)),
-        dma((1 + NZ,)),
+        dma((1 + TURNS,)),
+        dma((1 + TURNS,)),
+        dma((1 + TURNS,)),
+        dma((1 + TURNS,)),
+        dma((1 + TURNS,)),
         dma((1 + NZ,)),
     ]
-    return pl.pallas_call(
+    outs = pl.pallas_call(
         body,
         out_shape=(
             jax.ShapeDtypeStruct((2, D), BF),
@@ -721,6 +777,18 @@
         up_weight,
         down_weight,
     )
+    return pl.pallas_call(
+        hand_over,
+        out_shape=tuple(jax.ShapeDtypeStruct(v.shape, v.dtype) for v in outs),
+        in_specs=[vmem, vmem],
+        out_specs=(vmem, vmem),
+        name="hand_over",
+    )(*outs)
+
+
+def hand_over(mid, out, mid_to, out_to):
+    mid_to[...] = mid[...]
+    out_to[...] = out[...]
 
 
 def solution(mesh):

time: 100 us -> 92.4 us (0.924)
  Pallas kernels: 96.8 us -> 91.6 us
  local copies, waits for them, and re-layouts: 2.7 us -> 0 us
    pallas_call x1, Pallas kernels: 96.8 us -> 90.2 us  [local(): pl.pallas_call(body, out_shape=(jax.ShapeDtypeStruct((2, D), BF), jax.Sha...]
    unnamed x2 -> x0, local copies, waits for them, and re-layouts: 2.7 us -> none
    pallas_call x0 -> x1, Pallas kernels: none -> 1.37 us  [local(): pl.pallas_call(hand_over, out_shape=tuple((jax.ShapeDtypeStruct(v.shape,...]
where the time goes in v3:
time: 92.4 us; the launch traced here: 92.2 us
  Pallas kernels  91.6 us (99%)
    pallas_call x1, Pallas kernels, local(): pl.pallas_call(body, out_shape=(jax.ShapeDtypeStruct((2, D), BF), jax.Sha...  90.2 us

profile of v3, /device:TPU:1, one launch (start us, length us, event | category | flops | bytes accessed | tf_op | source)
XLA Modules:
  0.0 92.2 jit_solution(2995166429366347803)
XLA Ops:
  0.6 90.2 %layer.1 = (bf16[2,5376]{1,0:T(2,128)(2,1)}, bf16[16,672]{1,0:T(8,128)(2,1)}) custom-call(bf16[2,4096]{1,0:T(2,128)(2,1)} %refs_0_.1, bf16[2,2,2048]{2,1,0:T(2,128)(2,1)} %refs_1_.1, bf16[2,5376]{1,0:T(2,128)(2,1)} %refs_2_.1, f32[5376]{0:T(1024)} %refs_3_.1, f32[5376]{0:T(1024)} %refs_4_.1, s32[2]{0:T(128)} %refs_5_.1, s32[512]{0:T(512)} %refs_6_.1, ...), custom_call_target="tpu_custom_call" | custom-call | tf_op jit(solution)/shard_map/layer/pallas_call | solution.py:752
  90.8 1.4 %hand_over.1 = (bf16[2,5376]{1,0:T(2,128)(2,1)}, bf16[16,672]{1,0:T(8,128)(2,1)}) custom-call(bf16[2,5376]{1,0:T(2,128)(2,1)} %get-tuple-element.4.mid, bf16[16,672]{1,0:T(8,128)(2,1)} %get-tuple-element.5.out), custom_call_target="tpu_custom_call" | custom-call | tf_op jit(solution)/shard_map/hand_over/pallas_call | solution.py:780

commit v4 on v3

--- a/solution.py
+++ b/solution.py
@@ -20,13 +20,15 @@
 D = 5376
 CHUNKS = D // 128
 PROJ_ROWS = 88
+MAIN_ROWS = 72
+MAIN = 544
 BLOCK = 672
 SUF = 192
 SUFX = 208
 Y_OFFSETS = X_OFFSETS = (1, 3, 2)
 LAG = 6
 NEAR = (0, 1, 7, 2, 6, 3, 5, 4)
-FFN_ORDER = (0, 4, 2, 3, 6, 5, 1, 7)
+FFN_ORDER = (0, 1, 4, 7, 2, 6, 5, 3)
 FAR = (4, 5, 3, 6, 2, 7, 1, 0)
 TURNS = 4
 SCHEDULE = (
@@ -121,6 +123,10 @@
     precv,
     pzsend,
     pzrecv,
+    pbsend,
+    pbrecv,
+    pby,
+    pbyrecv,
     gains,
     resid,
     e1send,
@@ -129,6 +135,8 @@
     xf,
     xown,
     xall,
+    xby,
+    xallb,
     gu,
     gurecv,
     hid,
@@ -136,6 +144,10 @@
     yrecv,
     zsend,
     zrecv,
+    ybsend,
+    zbrecv,
+    yby,
+    ybyrecv,
     w_c,
     aq_z,
     aq_y,
@@ -145,13 +157,19 @@
     c_stz,
     d_y,
     d_z,
+    d_bz,
+    d_by,
     e_1,
     e_z,
     e_y,
+    e_by,
+    e_bz,
     f_x,
     f_hx,
     g_y,
     g_z,
+    g_bz,
+    g_by,
 ):
     me = lax.axis_index("prefix")
     spos = lax.axis_index("sample")
@@ -479,9 +497,15 @@
         for i in Y_OFFSETS + (0,):
             o = lax.rem(z + FAR[n], NZ) * NY + lax.rem(y + i, NY)
             start = pl.multiple_of(o * PROJ_ROWS, 8)
-            psend[n, i] = pf[pl.ds(start, PROJ_ROWS), :].astype(BF)
+            start_b = pl.multiple_of(o * PROJ_ROWS + MAIN_ROWS, 8)
+            psend[n, i] = pf[pl.ds(start, MAIN_ROWS), :].astype(BF)
+            pbsend[n, i] = pf[pl.ds(start_b, PROJ_ROWS - MAIN_ROWS), :].astype(BF)
             if i:
                 p_to_y(n, i)
+        if FAR[n]:
+            there = at_zy(lax.rem(z + FAR[n], NZ), y)
+            send(pbsend.at[n], pbrecv.at[n], d_bz, 1 + n, there)
+    all_left(pbrecv.at[pl.ds(0, NZ - 1)], d_bz)
     for n in (4, 5, 6):
         need(loads, n)
     for j in range(CHUNKS):
@@ -491,9 +515,22 @@
         gains[1, 2 * j : 2 * j + 2, :] = jnp.broadcast_to(fgain_ref[cols].reshape(1, 128), (2, 128))
     for n in range(NZ - 1):
         p_to_z(n, p_add_y(n))
+    rest = pbsend[NZ - 1].astype(F32)
+    for n in range(NZ - 1):
+        landed(pbrecv.at[n], d_bz, 1 + n)
+        rest = rest + pbrecv[n].astype(F32)
+    pby[...] = rest.astype(BF)
+    for i in Y_OFFSETS:
+        send(pby.at[i], pbyrecv.at[(-i) % NY], d_by, 1, at_zy(z, lax.rem(y + i, NY)))
+    all_left(pbyrecv.at[pl.ds(1, NY - 1)], d_by)
     projected = p_add_y(NZ - 1)
     for n in range(NZ - 1):
         projected = projected + p_add_z(n)
+    landed(pbyrecv.at[pl.ds(1, NY - 1)], d_by, 1)
+    rest = pby[0].astype(F32)
+    for i in Y_OFFSETS:
+        rest = rest + pbyrecv[i].astype(F32)
+    projected = jnp.concatenate([projected, rest], axis=0)
 
     row = lax.broadcasted_iota(jnp.int32, (PROJ_ROWS, 128), 0)
     odd = row % 2 == 1
@@ -539,8 +576,9 @@
         for i in range(6):
             for s in range(2):
                 xf[i, pl.ds(s, 8, stride=2), :] = e1f[pl.ds(2 * i + s, 8, stride=16), :]
-        for i in range(6):
-            xown[cc, :, i * 128 : (i + 1) * 128] = xf[i].astype(BF)
+        xby[0, cc] = xf[0].astype(BF)
+        for i in range(1, 6):
+            xown[cc, :, (i - 1) * 128 : i * 128] = xf[i].astype(BF)
 
     def turn(t):
         return FFN_ORDER[2 * t] * (1 - c) + FFN_ORDER[2 * t + 1] * c
@@ -553,6 +591,13 @@
             there = at_zy(z, lax.rem(y + i, NY))
             send(xall.at[t, 0], xall.at[t, (-i) % NY], e_y, 1 + t, there)
 
+    for i in Y_OFFSETS:
+        send(xby.at[0], xby.at[(-i) % NY], e_by, 1, at_zy(z, lax.rem(y + i, NY)))
+    all_left(xby.at[pl.ds(1, NY - 1)], e_by)
+
+    def xb_to_z(t):
+        send(xby, xallb.at[t], e_bz, 1 + t, at_zy(lax.rem(z + NZ - turn(t), NZ), y))
+
     for t in (3, 2, 1):
         x_to_z(t)
 
@@ -566,6 +611,18 @@
         landed(xall.at[0, 0], e_z, 1)
 
     x_to_y(0)
+    landed(xby.at[pl.ds(1, NY - 1)], e_by, 1)
+    for t in (3, 2, 1):
+        xb_to_z(t)
+
+    @pl.when(c == 0)
+    def _():
+        xallb[0] = xby[...]
+
+    @pl.when(c == 1)
+    def _():
+        xb_to_z(0)
+
     for t in range(1, TURNS):
         landed(xall.at[t, 0], e_z, 1 + t)
         x_to_y(t)
@@ -580,6 +637,7 @@
                 remote(sent, sent, sem.at[0], sem.at[0], at_xc(x, c)).wait_send()
 
     ending.append(lambda: some_left(xall.at[pl.ds(0, TURNS), 0], e_z))
+    ending.append(lambda: some_left(xallb, e_bz))
 
     for t in range(3):
         need(loads, 13 + t)
@@ -587,7 +645,18 @@
 
     def stage_a(t):
         landed(xall.at[t, pl.ds(1, NY - 1)], e_y, 1 + t)
-        v = [xall[t, :, cc].reshape(64, 768)[:, :BLOCK] for cc in range(NC)]
+        if t:
+            landed(xallb.at[t], e_bz, 1 + t)
+        else:
+
+            @pl.when(c == 1)
+            def _():
+                landed(xallb.at[0], e_bz, 1)
+
+        v = []
+        for cc in range(NC):
+            main = xall[t, :, cc].reshape(64, 640)[:, :MAIN]
+            v.append(jnp.concatenate([xallb[t, :, cc].reshape(64, 128), main], axis=1))
         for n in range(2):
             part = dot(v[0], ffw[n, 0]) + dot(v[1], ffw[n, 1])
             gu[t, :, n] = part.astype(BF).reshape(NY, 16, BLOCK)
@@ -609,10 +678,25 @@
         landed(hid.at[t, pl.ds(0, NX - 1)], f_hx, 1 + t)
         hidden = hid[t].reshape(64, BLOCK)
         for cc in range(NC):
-            ysend[t, :, cc] = dot(hidden, ffw[2, cc]).astype(BF).reshape(NY, 16, BLOCK)
+            down = dot(hidden, ffw[2, cc]).astype(BF)
+            ybsend[t, cc] = down[:, :128].reshape(NY, 16, 128)
+            ysend[t, :, cc] = down[:, 128:].reshape(NY, 16, MAIN)
         for i in Y_OFFSETS:
             there = at_zy(z, lax.rem(y + i, NY))
             send(ysend.at[t, i], yrecv.at[t, (-i) % NY], g_y, 1 + t, there)
+        to_cores(t, lambda n, cc, there: send(ybsend.at[t, cc], zbrecv.at[n], g_bz, 1 + n, there))
+
+    def to_cores(t, send_one):
+        zz = lax.rem(z + turn(t), NZ)
+        n = 2 * t + c
+        send_one(n, 1, at_zyc(zz, y, 1))
+        if t:
+            send_one(n, 0, at_zyc(zz, y, 0))
+        else:
+
+            @pl.when(c == 1)
+            def _():
+                send_one(n, 0, at_zyc(zz, y, 0))
 
     def stage_f(t):
         landed(yrecv.at[t, pl.ds(1, NY - 1)], g_y, 1 + t)
@@ -620,42 +704,41 @@
         for i in Y_OFFSETS:
             total = total + yrecv[t, i].astype(F32)
         zsend[t] = total.astype(BF)
-        zz = lax.rem(z + turn(t), NZ)
-        n = 2 * t + c
-
-        def to_core(cc):
-            send(zsend.at[t, cc], zrecv.at[n], g_z, 1 + n, at_zyc(zz, y, cc))
-
-        to_core(1)
-        if t:
-            to_core(0)
-        else:
-
-            @pl.when(c == 1)
-            def _():
-                to_core(0)
+        to_cores(t, lambda n, cc, there: send(zsend.at[t, cc], zrecv.at[n], g_z, 1 + n, there))
 
     all_left(gurecv.at[pl.ds(0, TURNS), pl.ds(1, NX - 1)], f_x)
     all_left(hid.at[pl.ds(0, TURNS), pl.ds(0, NX - 1)], f_hx)
     all_left(yrecv.at[pl.ds(0, TURNS), pl.ds(1, NY - 1)], g_y)
-    ending.append(lambda: some_left(zrecv, g_z))
     stages = {"a": stage_a, "c": stage_c, "e": stage_e, "f": stage_f}
     for name, t in SCHEDULE:
         stages[name](t)
 
-    @pl.when(c == 0)
-    def _():
-        zrecv[0] = zsend[0, 0]
-
-    @pl.when(c == 1)
-    def _():
-        landed(zrecv.at[0], g_z, 1)
-
-    total = zrecv[0].astype(F32)
-    for n in range(1, NZ):
-        landed(zrecv.at[n], g_z, 1 + n)
-        total = total + zrecv[n].astype(F32)
-    out_ref[...] = total.astype(BF)
+    def over_z(recv, own, sem):
+        @pl.when(c == 0)
+        def _():
+            recv[0] = own[...]
+
+        @pl.when(c == 1)
+        def _():
+            landed(recv.at[0], sem, 1)
+
+        total = recv[0].astype(F32)
+        for n in range(1, NZ):
+            landed(recv.at[n], sem, 1 + n)
+            total = total + recv[n].astype(F32)
+        ending.append(lambda: some_left(recv, sem))
+        return total
+
+    yby[...] = over_z(zbrecv, ybsend.at[0, 0], g_bz).astype(BF)
+    for i in Y_OFFSETS:
+        send(yby.at[i], ybyrecv.at[(-i) % NY], g_by, 1, at_zy(z, lax.rem(y + i, NY)))
+    all_left(ybyrecv.at[pl.ds(1, NY - 1)], g_by)
+    out_ref[:, 128:] = over_z(zrecv, zsend.at[0, 0], g_z).astype(BF)
+    landed(ybyrecv.at[pl.ds(1, NY - 1)], g_by, 1)
+    rest = yby[0].astype(F32)
+    for i in Y_OFFSETS:
+        rest = rest + ybyrecv[i].astype(F32)
+    out_ref[:, :128] = rest.astype(BF)
     out_copy = pltpu.make_async_copy(out_ref, out_hbm, out_sem.at[1])
     out_copy.start()
     ending.append(out_copy.wait)
@@ -713,25 +796,35 @@
         V((NZ, 8, 128), F32),
         V((NZ, 8, 128), F32),
         V((NP * PROJ_ROWS, 128), F32),
-        V((NZ, NY, PROJ_ROWS, 128), BF),
-        V((NZ, NY, PROJ_ROWS, 128), BF),
-        V((NZ, PROJ_ROWS, 128), BF),
-        V((NZ, PROJ_ROWS, 128), BF),
+        V((NZ, NY, MAIN_ROWS, 128), BF),
+        V((NZ, NY, MAIN_ROWS, 128), BF),
+        V((NZ, MAIN_ROWS, 128), BF),
+        V((NZ, MAIN_ROWS, 128), BF),
+        V((NZ, NY, 16, 128), BF),
+        V((NZ, NY, 16, 128), BF),
+        V((NY, 16, 128), BF),
+        V((NY, 16, 128), BF),
         V((2, PROJ_ROWS, 128), F32),
         V((PROJ_ROWS, 128), F32),
         V((NX, NC, 16, 128), BF),
         V((NS, NC, 16, 128), BF),
         V((NS * 16, 128), F32),
         V((6, 16, 128), F32),
-        V((NC, 16, 768), BF),
-        V((TURNS, NY, NC, 16, 768), BF),
+        V((NC, 16, 640), BF),
+        V((TURNS, NY, NC, 16, 640), BF),
+        V((NY, NC, 16, 128), BF),
+        V((TURNS, NY, NC, 16, 128), BF),
         V((TURNS, NX, 2, 16, BLOCK), BF),
         V((TURNS, NX, 2, 16, BLOCK), BF),
         V((TURNS, NX, 16, BLOCK), BF),
-        V((TURNS, NY, NC, 16, BLOCK), BF),
-        V((TURNS, NY, NC, 16, BLOCK), BF),
-        V((TURNS, NC, 16, BLOCK), BF),
-        V((NZ, 16, BLOCK), BF),
+        V((TURNS, NY, NC, 16, MAIN), BF),
+        V((TURNS, NY, NC, 16, MAIN), BF),
+        V((TURNS, NC, 16, MAIN), BF),
+        V((NZ, 16, MAIN), BF),
+        V((TURNS, NC, NY, 16, 128), BF),
+        V((NZ, NY, 16, 128), BF),
+        V((NY, 16, 128), BF),
+        V((NY, 16, 128), BF),
         dma((4,)),
         dma((1 + NZ,)),
         dma((1 + NZ,)),
@@ -741,13 +834,19 @@
         dma((1 + NZ,)),
         dma((1 + NZ,)),
         dma((1 + NZ,)),
+        dma((1 + NZ,)),
+        dma((2,)),
+        dma((2,)),
+        dma((1 + TURNS,)),
+        dma((1 + TURNS,)),
         dma((2,)),
         dma((1 + TURNS,)),
         dma((1 + TURNS,)),
         dma((1 + TURNS,)),
         dma((1 + TURNS,)),
-        dma((1 + TURNS,)),
-        dma((1 + NZ,)),
+        dma((1 + NZ,)),
+        dma((1 + NZ,)),
+        dma((2,)),
     ]
     outs = pl.pallas_call(
         body,

time: 92.4 us -> 89.3 us (0.966)
  Pallas kernels: 91.6 us -> 88.5 us
    pallas_call x1, Pallas kernels: 90.2 us -> 87.1 us  [local(): pl.pallas_call(body, out_shape=(jax.ShapeDtypeStruct((2, D), BF), jax.Sha...]
where the time goes in v4:
time: 89.3 us; the launch traced here: 89.1 us
  Pallas kernels  88.5 us (99%)
    pallas_call x1, Pallas kernels, local(): pl.pallas_call(body, out_shape=(jax.ShapeDtypeStruct((2, D), BF), jax.Sha...  87.1 us

profile of v4, /device:TPU:1, one launch (start us, length us, event | category | flops | bytes accessed | tf_op | source)
XLA Modules:
  0.0 89.1 jit_solution(13385878556792747779)
XLA Ops:
  0.6 87.1 %layer.1 = (bf16[2,5376]{1,0:T(2,128)(2,1)}, bf16[16,672]{1,0:T(8,128)(2,1)}) custom-call(bf16[2,4096]{1,0:T(2,128)(2,1)} %refs_0_.1, bf16[2,2,2048]{2,1,0:T(2,128)(2,1)} %refs_1_.1, bf16[2,5376]{1,0:T(2,128)(2,1)} %refs_2_.1, f32[5376]{0:T(1024)} %refs_3_.1, f32[5376]{0:T(1024)} %refs_4_.1, s32[2]{0:T(128)} %refs_5_.1, s32[512]{0:T(512)} %refs_6_.1, ...), custom_call_target="tpu_custom_call" | custom-call | tf_op jit(solution)/shard_map/layer/pallas_call | solution.py:851
  87.8 1.4 %hand_over.1 = (bf16[2,5376]{1,0:T(2,128)(2,1)}, bf16[16,672]{1,0:T(8,128)(2,1)}) custom-call(bf16[2,5376]{1,0:T(2,128)(2,1)} %get-tuple-element.4.mid, bf16[16,672]{1,0:T(8,128)(2,1)} %get-tuple-element.5.out), custom_call_target="tpu_custom_call" | custom-call | tf_op jit(solution)/shard_map/hand_over/pallas_call | solution.py:879

commit v5 on v4

--- a/solution.py
+++ b/solution.py
@@ -576,9 +576,9 @@
         for i in range(6):
             for s in range(2):
                 xf[i, pl.ds(s, 8, stride=2), :] = e1f[pl.ds(2 * i + s, 8, stride=16), :]
-        xby[0, cc] = xf[0].astype(BF)
+        xby[0, cc] = xf[0, 0:16].astype(BF)
         for i in range(1, 6):
-            xown[cc, :, (i - 1) * 128 : i * 128] = xf[i].astype(BF)
+            xown[cc, :, (i - 1) * 128 : i * 128] = xf[i, 0:16].astype(BF)
 
     def turn(t):
         return FFN_ORDER[2 * t] * (1 - c) + FFN_ORDER[2 * t + 1] * c
@@ -781,7 +781,7 @@
         dma((16,)),
         V((64, 128), F32),
         V((NZ, NY, 64, 128), BF),
-        V((NP * 64, 128), F32),
+        V((NP * 64 + 64, 128), F32),
         V((128, 128), F32),
         V((64, SUFX), F32),
         V((KV * 128, 128), F32),
@@ -795,7 +795,7 @@
         V((NZ, 64, 128), BF),
         V((NZ, 8, 128), F32),
         V((NZ, 8, 128), F32),
-        V((NP * PROJ_ROWS, 128), F32),
+        V((NP * PROJ_ROWS + PROJ_ROWS, 128), F32),
         V((NZ, NY, MAIN_ROWS, 128), BF),
         V((NZ, NY, MAIN_ROWS, 128), BF),
         V((NZ, MAIN_ROWS, 128), BF),
@@ -808,8 +808,8 @@
         V((PROJ_ROWS, 128), F32),
         V((NX, NC, 16, 128), BF),
         V((NS, NC, 16, 128), BF),
-        V((NS * 16, 128), F32),
-        V((6, 16, 128), F32),
+        V((NS * 16 + 16, 128), F32),
+        V((6, 24, 128), F32),
         V((NC, 16, 640), BF),
         V((TURNS, NY, NC, 16, 640), BF),
         V((NY, NC, 16, 128), BF),

time: 89.3 us -> 90.7 us (1.016)
  Pallas kernels: 88.5 us -> 89.9 us
    pallas_call x1, Pallas kernels: 87.1 us -> 88.5 us  [local(): pl.pallas_call(body, out_shape=(jax.ShapeDtypeStruct((2, D), BF), jax.Sha...]
where the time goes in v5:
time: 90.7 us; the launch traced here: 90.5 us
  Pallas kernels  89.9 us (99%)
    pallas_call x1, Pallas kernels, local(): pl.pallas_call(body, out_shape=(jax.ShapeDtypeStruct((2, D), BF), jax.Sha...  88.5 us

profile of v5, /device:TPU:1, one launch (start us, length us, event | category | flops | bytes accessed | tf_op | source)
XLA Modules:
  0.0 90.5 jit_solution(15872120240624237936)
XLA Ops:
  0.6 88.5 %layer.1 = (bf16[2,5376]{1,0:T(2,128)(2,1)}, bf16[16,672]{1,0:T(8,128)(2,1)}) custom-call(bf16[2,4096]{1,0:T(2,128)(2,1)} %refs_0_.1, bf16[2,2,2048]{2,1,0:T(2,128)(2,1)} %refs_1_.1, bf16[2,5376]{1,0:T(2,128)(2,1)} %refs_2_.1, f32[5376]{0:T(1024)} %refs_3_.1, f32[5376]{0:T(1024)} %refs_4_.1, s32[2]{0:T(128)} %refs_5_.1, s32[512]{0:T(512)} %refs_6_.1, ...), custom_call_target="tpu_custom_call" | custom-call | tf_op jit(solution)/shard_map/layer/pallas_call | solution.py:851
  89.1 1.4 %hand_over.1 = (bf16[2,5376]{1,0:T(2,128)(2,1)}, bf16[16,672]{1,0:T(8,128)(2,1)}) custom-call(bf16[2,5376]{1,0:T(2,128)(2,1)} %get-tuple-element.4.mid, bf16[16,672]{1,0:T(8,128)(2,1)} %get-tuple-element.5.out), custom_call_target="tpu_custom_call" | custom-call | tf_op jit(solution)/shard_map/hand_over/pallas_call | solution.py:879
